TPU v7x, 256 devices: a whole 4x4x8 slice. The times are simulated.
256 devices in a mesh: seq: 8 (over z), grp: 32 (over y, x, core).
Axes of the slice: x: 4, y: 4, z: 8, core: 2. Of those that a mesh axis runs over, the one named last changes fastest.
Arguments:
- history: bfloat16 [32, 1024, 512], P('grp', 'seq'), may hold values from -6 to 6
- lengths: int32 [32], P('grp'), may hold values from 256 to 1024, as said below
- next_items: int32 [32, 1024], P('grp', 'seq'), may hold values from 0 to 2047
- negatives: int32 [32, 512], P('grp'), may hold values from 0 to 2047
- input_weight: bfloat16 [512, 2048], replicated, may hold values from -0.25 to 0.25
- output_weight: bfloat16 [512, 512], replicated, may hold values from -0.25 to 0.25
- pool_features: bfloat16 [2048, 1024], P('grp'), may hold values from -6 to 6
- tower_first: bfloat16 [1024, 1024], P('grp'), may hold values from -0.1875 to 0.1875
- tower_middle: bfloat16 [1024, 1024], P('grp'), may hold values from -0.1875 to 0.1875
- tower_last: bfloat16 [1024, 512], P('grp'), may hold values from -0.1875 to 0.1875
Outputs:
- layer_out: bfloat16 [32, 1024, 512], P('grp', 'seq')
- loss: float32 [], replicated
- user_grad: float32 [32, 1024, 512], P('grp', 'seq')
- grad_first: float32 [1024, 1024], P('grp')
- grad_middle: float32 [1024, 1024], P('grp')
- grad_last: float32 [1024, 512], P('grp')
Inputs may be any that keep to these rules, and one draw needn't show every extreme that they name: `lengths`: each user's history holds 256 to 1024 events; in every draw one user has exactly 1024 and another exactly 256.
All inputs are finite; a program needn't handle non-finite values.
Results may differ from a plain program's by a relative error of at most 0.017.
Values may be sent and summed in bfloat16 or wider, within the bound.
A program may use at most 64 MiB of HBM per device.

v0:
```python
import jax
import jax.numpy as jnp
from jax import lax
from jax.sharding import PartitionSpec as P

H = 8
DH = 64


epsilon_norm = 1e-05
epsilon_unit = 1e-06
inverse_temp = 20.0


def layer_norm(values):
    center = values - jnp.mean(values, axis=-1, keepdims=True)
    spread = jnp.mean(center * center, axis=-1, keepdims=True)
    return center * lax.rsqrt(spread + epsilon_norm)


def silu_slope(preact):
    sigma = jax.nn.sigmoid(preact)
    return sigma * (1.0 + preact * (1.0 - sigma))


def tower_forward(features, first_weight, middle_weight, last_weight):
    pre_first = jnp.dot(features, first_weight, preferred_element_type=jnp.float32)
    hidden_first = jax.nn.silu(pre_first).astype(jnp.bfloat16)
    pre_second = jnp.dot(hidden_first, middle_weight, preferred_element_type=jnp.float32)
    hidden_second = jax.nn.silu(pre_second).astype(jnp.bfloat16)
    raw_item = jnp.dot(hidden_second, last_weight, preferred_element_type=jnp.float32)
    item_inverse = lax.rsqrt(jnp.sum(raw_item * raw_item, axis=-1, keepdims=True) + epsilon_unit)
    return (
        pre_first,
        hidden_first,
        pre_second,
        hidden_second,
        raw_item * item_inverse,
        item_inverse,
    )


def sample_loss(layer_out, length, items, negative_row, pool_emb, positions):
    outward = layer_out.astype(jnp.float32)
    user_inverse = lax.rsqrt(jnp.sum(outward * outward, axis=-1, keepdims=True) + epsilon_unit)
    unit_user = outward * user_inverse
    unit_low = unit_user.astype(jnp.bfloat16)
    positive_rows = jnp.take(pool_emb, items, axis=0)
    negative_rows = jnp.take(pool_emb, negative_row, axis=0)
    positive_logit = inverse_temp * jnp.sum(
        unit_low.astype(jnp.float32) * positive_rows.astype(jnp.float32), axis=-1
    )
    negative_logit = inverse_temp * jnp.dot(
        unit_low, negative_rows.T, preferred_element_type=jnp.float32
    )
    kept = (negative_row[None, :] != items[:, None]).astype(jnp.float32)
    positive_exp = jnp.exp(positive_logit)
    negative_exp = jnp.exp(negative_logit) * kept
    denominator = positive_exp + jnp.sum(negative_exp, axis=-1)
    valid = (positions < length - 1).astype(jnp.float32)
    token_loss = jnp.log(denominator) - positive_logit
    loss_sum = jnp.sum(valid * token_loss)
    positive_slope = valid * (positive_exp / denominator - 1.0)
    negative_slope = (valid[:, None] * negative_exp / denominator[:, None]).astype(jnp.bfloat16)
    user_dir = inverse_temp * (
        positive_slope[:, None] * positive_rows.astype(jnp.float32)
        + jnp.dot(negative_slope, negative_rows, preferred_element_type=jnp.float32)
    )
    user_grad = user_inverse * (
        user_dir - unit_user * jnp.sum(unit_user * user_dir, axis=-1, keepdims=True)
    )
    pool_term = jnp.zeros((pool_emb.shape[0], pool_emb.shape[1]), jnp.float32)
    pool_term = pool_term.at[items].add(
        inverse_temp * positive_slope[:, None] * unit_low.astype(jnp.float32)
    )
    negative_part = lax.dot_general(
        negative_slope, unit_low, (((0,), (0,)), ((), ())), preferred_element_type=jnp.float32
    )
    pool_term = pool_term.at[negative_row].add(inverse_temp * negative_part)
    return (loss_sum, user_grad, pool_term)


def block_term(queries, query_pos, key_block, value_block, key_pos, length):
    scores = jnp.einsum(
        "qhd,khd->hqk", queries, key_block, preferred_element_type=jnp.float32
    ) * DH ** (-0.5)
    allowed = (
        (key_pos[None, :] <= query_pos[:, None])
        & (key_pos[None, :] < length)
        & (query_pos[:, None] < length)
    )
    weights = jnp.where(allowed[None], jax.nn.silu(scores), 0.0) / length.astype(jnp.float32)
    weights = weights.astype(jnp.bfloat16)
    return jnp.einsum("hqk,khd->qhd", weights, value_block, preferred_element_type=jnp.float32)


def attend_whole(mixed_heads, length):
    full_len = mixed_heads.shape[0]
    head_count = mixed_heads.shape[1]
    width = min(512, full_len)
    live_blocks = (length + width - 1) // width

    def query_step(block_index, result):
        first_row = block_index * width
        queries = lax.dynamic_slice_in_dim(mixed_heads, first_row, width, 0)[..., :DH]
        query_pos = first_row + jnp.arange(width, dtype=jnp.int32)

        def key_step(column, running):
            key_first = column * width
            key_rows = lax.dynamic_slice_in_dim(mixed_heads, key_first, width, 0)
            key_pos = key_first + jnp.arange(width, dtype=jnp.int32)
            return running + block_term(
                queries,
                query_pos,
                key_rows[..., DH : 2 * DH],
                key_rows[..., 2 * DH :],
                key_pos,
                length,
            )

        running = lax.fori_loop(
            0, block_index + 1, key_step, jnp.zeros((width, head_count, DH), jnp.float32)
        )
        return lax.dynamic_update_slice_in_dim(result, running.astype(jnp.bfloat16), first_row, 0)

    return lax.fori_loop(
        0, live_blocks, query_step, jnp.zeros((full_len, head_count, DH), jnp.bfloat16)
    )


def outer_sum(left, right):
    return lax.psum_scatter(
        lax.dot_general(left, right, (((0,), (0,)), ((), ())), preferred_element_type=jnp.float32),
        "grp",
        scatter_dimension=0,
        tiled=True,
    )


def local(
    history,
    lengths,
    next_items,
    negatives,
    input_weight,
    output_weight,
    pool_features,
    tower_first,
    tower_middle,
    tower_last,
):
    events = history[0]
    tok_count = events.shape[0]
    length = lengths[0]
    hidden_width = output_weight.shape[0]
    offset = lax.axis_index("seq") * tok_count
    positions = offset + jnp.arange(tok_count, dtype=jnp.int32)
    normed = layer_norm(events.astype(jnp.float32)).astype(jnp.bfloat16)
    projected = jax.nn.silu(
        jnp.dot(normed, input_weight, preferred_element_type=jnp.float32)
    ).astype(jnp.bfloat16)
    gate = projected[:, :hidden_width]
    mixed_heads = projected[:, hidden_width:].reshape(tok_count, H, 3 * DH)
    regrouped = lax.all_to_all(mixed_heads, "seq", split_axis=1, concat_axis=0, tiled=True)
    head_result = attend_whole(regrouped, length)
    attended = lax.all_to_all(head_result, "seq", split_axis=0, concat_axis=1, tiled=True)
    merged = attended.reshape(tok_count, hidden_width).astype(jnp.float32)
    branch = (layer_norm(merged) * gate.astype(jnp.float32)).astype(jnp.bfloat16)
    layer_out = (
        events.astype(jnp.float32)
        + jnp.dot(branch, output_weight, preferred_element_type=jnp.float32)
    ).astype(jnp.bfloat16)
    full_first, full_middle, full_last = (
        lax.all_gather(tower_first, "grp", axis=0, tiled=True),
        lax.all_gather(tower_middle, "grp", axis=0, tiled=True),
        lax.all_gather(tower_last, "grp", axis=0, tiled=True),
    )
    pre_first, hidden_first, pre_second, hidden_second, unit_item, item_inverse = tower_forward(
        pool_features, full_first, full_middle, full_last
    )
    pool_emb = lax.all_gather(unit_item.astype(jnp.bfloat16), "grp", axis=0, tiled=True)
    loss_sum, user_grad, pool_term = sample_loss(
        layer_out, length, next_items[0], negatives[0], pool_emb, positions
    )
    count_term = jnp.where(lax.axis_index("seq") == 0, length - 1, 0).astype(jnp.float32)
    loss_parts = lax.psum((loss_sum, count_term), ("seq", "grp"))
    loss = loss_parts[0] / loss_parts[1]
    owned_part = lax.psum_scatter(pool_term, "grp", scatter_dimension=0, tiled=True)
    own_grad = lax.psum(owned_part, "seq")
    raw_grad = (
        item_inverse
        * (own_grad - unit_item * jnp.sum(unit_item * own_grad, axis=-1, keepdims=True))
    ).astype(jnp.bfloat16)
    grad_last = outer_sum(hidden_second, raw_grad)
    second_grad = (
        jnp.dot(raw_grad, full_last.T, preferred_element_type=jnp.float32) * silu_slope(pre_second)
    ).astype(jnp.bfloat16)
    grad_middle = outer_sum(hidden_first, second_grad)
    first_grad = (
        jnp.dot(second_grad, full_middle.T, preferred_element_type=jnp.float32)
        * silu_slope(pre_first)
    ).astype(jnp.bfloat16)
    grad_first = outer_sum(pool_features, first_grad)
    return (layer_out[None], loss, user_grad[None], grad_first, grad_middle, grad_last)


def solution(mesh):
    placed = (
        P("grp", "seq", None),
        P("grp"),
        P("grp", "seq"),
        P("grp", None),
        P(),
        P(),
        P("grp", None),
        P("grp", None),
        P("grp", None),
        P("grp", None),
    )
    return jax.shard_map(
        local,
        mesh=mesh,
        in_specs=placed,
        out_specs=(
            P("grp", "seq", None),
            P(),
            P("grp", "seq", None),
            P("grp", None),
            P("grp", None),
            P("grp", None),
        ),
        check_vma=False,
    )
```

profile of v0, /device:TPU:1, one launch (start us, length us, event | category | flops | bytes accessed | tf_op | source)
XLA Modules:
  0.0 684.1 jit_solution(15431327799769288946)
XLA Ops:
  7.2 0.7 all-gather.5.cloned.1.call-update
  8.0 0.7 all-gather.7.cloned.1.call-update
  8.7 0.7 all-gather.9.cloned.1.call-update
  9.4 1.0 convert_reduce_fusion
  10.4 1.1 fusion.36
  11.5 1.5 multiply_convert_fusion
  13.0 0.8 copy-done.6
  13.8 0.9 copy.35
  14.8 9.0 %all-to-all-start = ((bf16[128,8,192]{0,2,1:T(8,128)(2,1)}), bf16[128,8,192]{0,2,1:T(8,128)(2,1)S(1)}, u32[]{:S(2)}, u32[]{:S(2)}) async-start(bf16[128,8,192]{0,2,1:T(8,128)(2,1)} %bitcast.2), calls=%async_computation | async-start | bytes 786432 | tf_op jit(solution)/shard_map/all_to_all | solution.py:164
  25.1 12.9 %all-to-all-done = bf16[128,8,192]{0,2,1:T(8,128)(2,1)S(1)} async-done(((bf16[128,8,192]{0,2,1:T(8,128)(2,1)}), bf16[128,8,192]{0,2,1:T(8,128)(2,1)S(1)}, u32[]{:S(2)}, u32[]{:S(2)}) %all-to-all-start) | async-done | bytes 393248 | tf_op jit(solution)/shard_map/all_to_all | solution.py:164
  38.1 25.6 %all-gather.5.cloned.1.call-done = bf16[1024,1024]{1,0:T(8,128)(2,1)} async-done(((bf16[32,1024]{1,0:T(8,128)(2,1)}), bf16[1024,1024]{1,0:T(8,128)(2,1)}) %all-gather.5.cloned.1.call-update) | async-done | bytes 2097168 | tf_op jit(solution)/shard_map/all_gather | solution.py:174
  63.7 2.1 fusion.72
  65.8 48.6 %all-gather.7.cloned.1.call-done = bf16[1024,1024]{1,0:T(8,128)(2,1)} async-done(((bf16[32,1024]{1,0:T(8,128)(2,1)}), bf16[1024,1024]{1,0:T(8,128)(2,1)}) %all-gather.7.cloned.1.call-update) | async-done | bytes 2097168 | tf_op jit(solution)/shard_map/all_gather | solution.py:175
  114.4 2.1 fusion.68
  116.5 47.6 %all-gather.9.cloned.1.call-done = bf16[1024,512]{1,0:T(8,128)(2,1)} async-done(((bf16[32,512]{1,0:T(8,128)(2,1)}), bf16[1024,512]{1,0:T(8,128)(2,1)}) %all-gather.9.cloned.1.call-update) | async-done | bytes 1048592 | tf_op jit(solution)/shard_map/all_gather | solution.py:176
  164.1 1.6 multiply_reduce_fusion.2
  165.7 0.7 multiply_convert_fusion.6
  166.5 1.6 while.26
  166.6 1.5 while.27
  167.3 0.8 fusion.90
  169.5 0.9 reshape.248
  170.4 6.7 all-to-all-start.1
  178.3 6.8 %all-to-all-done.1 = bf16[8,2,4096]{2,1,0:T(2,128)(2,1)S(1)} async-done(((bf16[8,2,4096]{2,1,0:T(2,128)(2,1)}), bf16[8,2,4096]{2,1,0:T(2,128)(2,1)S(1)}, u32[]{:S(2)}, u32[]{:S(2)}) %all-to-all-start.1) | async-done | bytes 131104 | tf_op jit(solution)/shard_map/all_to_all | solution.py:166
  185.8 0.8 copy.39
  186.5 1.8 copy.40
  188.3 2.2 convert_reduce_fusion.1
  190.6 1.6 fusion.42
  192.2 23.1 %all-gather.11.cloned.1.call-done = bf16[2048,512]{1,0:T(8,128)(2,1)} async-done(((bf16[64,512]{1,0:T(8,128)(2,1)}), bf16[2048,512]{1,0:T(8,128)(2,1)}) %all-gather.11.cloned.1.call-update) | async-done | bytes 2097168 | tf_op jit(solution)/shard_map/all_gather | solution.py:181
  215.3 2.7 gather_fusion
  218.1 0.8 fusion.43
  218.9 4.5 gather_fusion.1
  223.5 1.5 fusion.71
  225.6 3.7 scatter_custom_fusion
  229.3 1.4 convolution_multiply_fusion.1
  230.8 8.3 %scatter_fusion = f32[2048,512]{1,0:T(8,128)} fusion(f32[2048,512]{1,0:T(8,128)} %scatter_custom_fusion, s32[512]{0:T(512)S(1)} %bitcast.103, f32[512,512]{1,0:T(8,128)} %convolution_multiply_fusion.1), kind=kCustom, calls=%fused_computation.3 | custom fusion | flops 262144 | bytes 3147776 | tf_op jit(solution)/shard_map/scatter-add | solution.py:79
  239.2 86.8 %reduce-scatter.7.cloned.1.call-done = f32[64,512]{1,0:T(8,128)} async-done(((f32[2048,512]{1,0:T(8,128)}), f32[64,512]{1,0:T(8,128)}) %reduce-scatter.7.cloned.1.call-update) | async-done | bytes 131088 | tf_op jit(solution)/shard_map/reduce_scatter | solution.py:188
  326.1 70.2 %all-reduce.3.cloned.1.call-done = f32[64,512]{1,0:T(8,128)} async-done(((f32[64,512]{1,0:T(8,128)}), f32[64,512]{1,0:T(8,128)}) %all-reduce.3.cloned.1.call-update) | async-done | bytes 131088 | tf_op jit(solution)/shard_map/psum | solution.py:189
  396.2 1.1 multiply_reduce_fusion.1
  397.3 1.0 multiply_convert_fusion.5
  398.3 1.8 fusion.69
  400.2 1.7 fusion.29
  401.9 4.9 convolution_bitcast_fusion.1
  406.8 5.3 copy.42
  412.2 2.7 fusion.67
  415.0 80.1 %all-reduce = (f32[]{:T(128)}, f32[]{:T(128)}) all-reduce(f32[]{:T(128)} %get-tuple-element.220, f32[]{:T(128)S(6)} %convert_element_type.125), channel_id=1, replica_groups=mesh['seq'=8,'grp'=32] {'seq','grp'}, use_global_device_ids=true, to_apply=%region_14.15 | all-reduce | flops 2 | bytes 16 | tf_op jit(solution)/shard_map/psum | solution.py:186
  496.8 0.8 fusion.41
  497.6 84.8 %reduce-scatter.13.cloned.1.call-done = f32[32,1024]{1,0:T(8,128)} async-done(((f32[1024,1024]{1,0:T(8,128)}), f32[32,1024]{1,0:T(8,128)}) %reduce-scatter.13.cloned.1.call-update) | async-done | bytes 131088
  582.4 94.0 %reduce-scatter.9.cloned.1.call-done = f32[32,1024]{1,0:T(8,128)} async-done(((f32[1024,1024]{1,0:T(8,128)}), f32[32,1024]{1,0:T(8,128)}) %reduce-scatter.9.cloned.1.call-update) | async-done | bytes 131088 | tf_op jit(solution)/shard_map/reduce_scatter | solution.py:132
  (83 shorter events, 6.1 us)
Async XLA Ops:
  7.2 4.4 copy-start
  7.2 56.5 %all-gather.5.cloned.1.call-start = ((), (), s32[]{:S(2)}) async-start(), calls=%async_computation.6 | async-start | bytes 2162688 | tf_op jit(solution)/shard_map/all_gather | solution.py:174
  7.9 106.5 %all-gather.7.cloned.1.call-start = ((), (), s32[]{:S(2)}) async-start(), calls=%async_computation.7 | async-start | bytes 2162688 | tf_op jit(solution)/shard_map/all_gather | solution.py:175
  8.7 155.4 %all-gather.9.cloned.1.call-start = ((), (), s32[]{:S(2)}) async-start(), calls=%async_computation.8 | async-start | bytes 1081344 | tf_op jit(solution)/shard_map/all_gather | solution.py:176
  13.0 0.8 copy-start.6
  13.8 10.0 %copy-start.8 = (s32[1,512]{1,0:T(1,128)S(1)}, s32[1,512]{1,0:T(1,128)}, u32[]{:S(2)}) copy-start(s32[1,512]{1,0:T(1,128)} %param.17) | copy-start | bytes 6148
  13.8 10.7 %copy-start.14 = (s32[1,128]{1,0:T(1,128)S(1)}, s32[1,128]{1,0:T(1,128)}, u32[]{:S(2)}) copy-start(s32[1,128]{1,0:T(1,128)} %param.16) | copy-start | bytes 1540
  13.8 49.9 %copy-start.7 = (bf16[64,1024]{1,0:T(8,128)(2,1)S(1)}, bf16[64,1024]{1,0:T(8,128)(2,1)}, u32[]{:S(2)}) copy-start(bf16[64,1024]{1,0:T(8,128)(2,1)} %param.20) | copy-start | bytes 393220
  14.8 23.3 %all-to-all-start = ((bf16[128,8,192]{0,2,1:T(8,128)(2,1)}), bf16[128,8,192]{0,2,1:T(8,128)(2,1)S(1)}, u32[]{:S(2)}, u32[]{:S(2)}) async-start(bf16[128,8,192]{0,2,1:T(8,128)(2,1)} %bitcast.2), calls=%async_computation | async-start | bytes 786432 | tf_op jit(solution)/shard_map/all_to_all | solution.py:164
  23.8 191.6 %all-gather.11.cloned.1.call-start = ((), (), s32[]{:S(2)}) async-start(), calls=%async_computation.9 | async-start | bytes 2162688 | tf_op jit(solution)/shard_map/all_gather | solution.py:181
  24.6 91.9 %copy-start.12 = (s32[128]{0:T(128)}, s32[128]{0:T(128)S(1)}, u32[]{:S(2)}) copy-start(s32[128]{0:T(128)S(1)} %fusion.59) | copy-start | bytes 1540
  116.5 50.0 %copy-start.3 = (f32[64,1024]{1,0:T(8,128)}, f32[64,1024]{1,0:T(8,128)S(1)}, u32[]{:S(2)}) copy-start(f32[64,1024]{1,0:T(8,128)S(1)} %fusion.68) | copy-start | bytes 786436
  165.7 0.7 copy-start.9
  169.4 21.3 %copy-start.2 = (bf16[1,128,512]{2,1,0:T(8,128)(2,1)S(1)}, bf16[1,128,512]{2,1,0:T(8,128)(2,1)}, u32[]{:S(2)}) copy-start(bf16[1,128,512]{2,1,0:T(8,128)(2,1)} %param.14) | copy-start | bytes 393220
  170.4 14.7 %all-to-all-start.1 = ((bf16[8,2,4096]{2,1,0:T(2,128)(2,1)}), bf16[8,2,4096]{2,1,0:T(2,128)(2,1)S(1)}, u32[]{:S(2)}, u32[]{:S(2)}) async-start(bf16[8,2,4096]{2,1,0:T(2,128)(2,1)} %reshape.248), calls=%async_computation.1 | async-start | bytes 262144 | tf_op jit(solution)/shard_map/all_to_all | solution.py:166
  177.2 148.8 %reduce-scatter.7.cloned.1.call-start = ((), (), s32[]{:S(2)}) async-start(), calls=%async_computation.10 | async-start | bytes 4325376 | tf_op jit(solution)/shard_map/reduce_scatter | solution.py:188
  192.2 304.6 %copy-start.1 = (bf16[128,512]{1,0:T(8,128)(2,1)}, bf16[128,512]{1,0:T(8,128)(2,1)S(1)}, u32[]{:S(2)}) copy-start(bf16[128,512]{1,0:T(8,128)(2,1)S(1)} %get-tuple-element.226) | copy-start | bytes 393220
  218.9 4.6 copy-start.13
  218.9 4.5 copy-start.15
  225.0 4.3 copy-start.16
  225.6 3.7 copy-start.18
  239.1 157.2 %copy-start.10 = (f32[64]{0:T(128)S(1)}, f32[64]{0:T(128)}, u32[]{:S(2)}) copy-start(f32[64]{0:T(128)} %copy-done.9) | copy-start | bytes 772
  239.1 159.3 %copy-start.4 = (f32[64,1024]{1,0:T(8,128)S(1)}, f32[64,1024]{1,0:T(8,128)}, u32[]{:S(2)}) copy-start(f32[64,1024]{1,0:T(8,128)} %copy-done.3) | copy-start | bytes 786436
  239.1 157.1 %all-reduce.3.cloned.1.call-start = ((), (), s32[]{:S(2)}) async-start(), calls=%async_computation.11 | async-start | bytes 262144 | tf_op jit(solution)/shard_map/psum | solution.py:189
  326.0 171.6 %reduce-scatter.11.cloned.1.call-start = ((), (), s32[]{:S(2)}) async-start(), calls=%async_computation.13 | async-start | bytes 2162688 | tf_op jit(solution)/shard_map/reduce_scatter | solution.py:132
  400.1 182.3 %reduce-scatter.13.cloned.1.call-start = ((), (), s32[]{:S(2)}) async-start(), calls=%async_computation.14 | async-start | bytes 4325376
  412.2 264.3 %reduce-scatter.9.cloned.1.call-start = ((), (), s32[]{:S(2)}) async-start(), calls=%async_computation.12 | async-start | bytes 4325376 | tf_op jit(solution)/shard_map/reduce_scatter | solution.py:132
  414.9 81.4 %copy-start.5 = (bf16[512,512]{1,0:T(8,128)(2,1)S(1)}, bf16[512,512]{1,0:T(8,128)(2,1)}, u32[]{:S(2)}) copy-start(bf16[512,512]{1,0:T(8,128)(2,1)} %gather_fusion.1) | copy-start | bytes 1572868
  414.9 81.4 %copy-start.11 = (pred[128]{0:T(512)(128)(4,1)S(1)}, pred[128]{0:T(512)(128)(4,1)}, u32[]{:S(2)}) copy-start(pred[128]{0:T(512)(128)(4,1)} %compare_and_fusion.1) | copy-start | bytes 388
  414.9 81.4 %copy-start.17 = (f32[128,512]{1,0:T(8,128)S(1)}, f32[128,512]{1,0:T(8,128)}, u32[]{:S(2)}) copy-start(f32[128,512]{1,0:T(8,128)} %copy-done.16) | copy-start | bytes 786436
Sparse Core Ops, SparseCore 0:
  10.6 53.0 all-gather.4
  66.3 48.1 all-gather.6
  117.0 47.0 all-gather.8
  167.1 48.2 all-gather.10
  239.2 86.7 reduce-scatter.6
  328.3 67.9 all-reduce.2
  400.6 88.2 reduce-scatter.10
  493.5 88.9 reduce-scatter.12
  587.5 88.9 reduce-scatter.8
where the time goes:
time: 686 us; the launch traced here: 684 us
  waiting for transfers between devices  503 us (73%)
  blocking collectives  80.1 us (12%)
  other arithmetic  24.4 us (4%)
  matrix products  24.1 us (4%)
  local copies, waits for them, and re-layouts  19.3 us (3%)
  between operations  17.3 us (3%)
  starting transfers between devices  16.1 us (2%)
    reduce_scatter x2, waiting for transfers between devices, outer_sum(): lax.psum_scatter(lax.dot_general(left, right, (((0,), (0,)), ((), ())), p...  94 us
    unnamed x10, waiting for transfers between devices  87 us
    reduce_scatter x1, waiting for transfers between devices, local(): lax.psum_scatter(pool_term, 'grp', scatter_dimension=0, tiled=True)  86.8 us
    psum x1, blocking collectives, local(): loss_parts = lax.psum((loss_sum, count_term), ('seq', 'grp'))  80.1 us
    psum x1, waiting for transfers between devices, local(): own_grad = lax.psum(owned_part, 'seq')  70.2 us
    all_gather x1, waiting for transfers between devices, local(): lax.all_gather(tower_middle, 'grp', axis=0, tiled=True)  48.6 us
    all_gather x1, waiting for transfers between devices, local(): lax.all_gather(tower_last, 'grp', axis=0, tiled=True)  47.6 us
    all_gather x1, waiting for transfers between devices, local(): lax.all_gather(tower_first, 'grp', axis=0, tiled=True)  25.6 us
  transfers between devices with their start and end apart: 11, of which 10 were waited for; matrix products, arithmetic and copies ran while one was open for 5% of the time, Pallas kernels for 0%

commit v1 on v0

v1 whole, which is shorter than its diff:
```python
import functools

import jax
import jax.numpy as jnp
from jax import lax
from jax.experimental import pallas as pl
from jax.experimental.pallas import tpu as pltpu
from jax.sharding import PartitionSpec as P

DH = 64
EPS_NORM = 1e-05
EPS_UNIT = 1e-06
TEMP = 20.0

MESH = pl.DeviceIdType.MESH
BF = jnp.bfloat16
F32 = jnp.float32

A, B, AS, BS, QKV, ATT, H1, H2, PES, ZR, ZG, PP, G1, G2, F1, F2, RS = range(17)
PE, PAIR = 17, 20
N_SEM = 24


def silu(x):
    half = 0.5 * x
    return half * (1.0 + jnp.tanh(half))


def silu_slope(z):
    sigma = 0.5 * (1.0 + jnp.tanh(0.5 * z))
    return sigma * (1.0 + z * (1.0 - sigma))


def layer_norm(values):
    center = values - jnp.mean(values, axis=-1, keepdims=True)
    spread = jnp.mean(center * center, axis=-1, keepdims=True)
    return center * lax.rsqrt(spread + EPS_NORM)


def dot(a, b):
    return jnp.dot(a, b, preferred_element_type=F32)


def dot_t(a, b):
    return lax.dot_general(a, b, (((1,), (1,)), ((), ())), preferred_element_type=F32)


def t_dot(a, b):
    return lax.dot_general(a, b, (((0,), (0,)), ((), ())), preferred_element_type=F32)


def wait(ref, sem):
    pltpu.make_async_copy(ref, ref, sem).wait()


def kernel(
    S, G,
    len_ref, hist, nxt, neg, win, wout, xf, w1, w2, w3,
    lo_ref, loss_ref, ug_ref, gf_ref, gm_ref, gl_ref,
    send, recv,
    a_buf, b_buf, qs_buf, qr_buf, gate, k_scr, q_scr, v_scr, at_send, at_recv,
    h1_buf, h2_buf, pre1, pre2, ui, inv, pe_buf, em, sl, pt_send, pair_recv, rs_send, rs_recv,
    zs_send, zs_recv, zg_buf, rg, p_send, p_recv, gl_scr, g1_send, g1_recv, g2_send, g2_recv,
    f1_buf, f2_buf, cnt, uu, uinv,
):
    C = G // 2
    s = lax.axis_index("seq")
    g = lax.axis_index("grp")
    p = g // 2
    c = g % 2
    tok = hist.shape[0]
    length = len_ref[0]

    def z_partner(k):
        return lax.rem(s + k, S)

    def copy(src, dst, i, dev, j=None):
        return pltpu.make_async_remote_copy(
            src_ref=src, dst_ref=dst, send_sem=send.at[i if j is None else j],
            recv_sem=recv.at[i if j is None else j], device_id=dev, device_id_type=MESH)

    def z_bcast(buf, i):
        def step(k, _):
            copy(buf.at[s], buf.at[s], i, (z_partner(k), g)).start()
            return 0
        lax.fori_loop(1, S, step, 0)

    def z_scatter(src, dst, i):
        def step(k, _):
            t = z_partner(k)
            copy(src.at[t], dst.at[s], i, (t, g)).start()
            return 0
        lax.fori_loop(1, S, step, 0)

    def grp_scatter(src, dst, i):
        def step(k, _):
            t = lax.rem(g + k, G)
            copy(src.at[t], dst.at[g], i, (s, t)).start()
            return 0
        lax.fori_loop(1, G, step, 0)

    barrier = pltpu.get_barrier_semaphore()

    def greet_grp(k, _):
        pl.semaphore_signal(barrier, inc=1, device_id=(s, lax.rem(g + k, G)), device_id_type=MESH)
        return 0

    def greet_seq(k, _):
        pl.semaphore_signal(barrier, inc=1, device_id=(z_partner(k), g), device_id_type=MESH)
        return 0

    lax.fori_loop(1, G, greet_grp, 0)
    lax.fori_loop(1, S, greet_seq, 0)

    cols = pl.ds(pl.multiple_of(s * 128, 128), 128)
    rows = w1.shape[0]
    a_buf[p, c, :rows] = w1[:, cols]
    a_buf[p, c, rows:] = w2[:, cols]
    b_buf[p, c] = w3[...]
    pl.semaphore_wait(barrier, (G - 1) + (S - 1))

    def a_step(k, _):
        t = lax.rem(p + k, C)
        copy(a_buf.at[p, c], a_buf.at[p, c], A, (s, 2 * t + c)).start()
        return 0

    lax.fori_loop(1, C, a_step, 0)

    events = hist[...].astype(F32)
    normed = layer_norm(events).astype(BF)
    gate[...] = silu(dot(normed, win[:, :512])).astype(BF)
    for j in range(4):
        x = silu(dot(normed, win[:, 512 + 384 * j : 512 + 384 * (j + 1)])).astype(BF)
        for e in (0, 1):
            o = 192 * e
            qs_buf[2 * j + e, :tok] = x[:, o : o + 128]
            v = x[:, o + 128 : o + 192]
            qs_buf[2 * j + e, tok:] = jnp.concatenate([v[: tok // 2], v[tok // 2 :]], axis=1)
    z_scatter(qs_buf, qr_buf, QKV)
    qr_buf[s] = qs_buf[s]

    def b_step(k, _):
        t = lax.rem(p + k, C)
        copy(b_buf.at[p, c], b_buf.at[p, c], B, (s, 2 * t + c)).start()
        return 0

    lax.fori_loop(1, C, b_step, 0)

    sib = (s, 2 * p + 1 - c)
    wait(a_buf.at[pl.ds(0, C - 1), 0], recv.at[A])
    copy(a_buf.at[:, c], a_buf.at[:, c], AS, sib).start()

    ids = neg[...]
    n_hi = cnt.shape[0]
    oh_hi = (lax.broadcasted_iota(jnp.int32, (n_hi, ids.shape[1]), 0) == (ids >> 7)).astype(F32).astype(BF)
    oh_lo = (lax.broadcasted_iota(jnp.int32, (128, ids.shape[1]), 0) == (ids & 127)).astype(F32).astype(BF)
    cnt[...] = dot_t(oh_hi, oh_lo)

    wait(a_buf.at[:, 0], recv.at[AS])
    x_own = xf[...]
    z1 = dot(x_own, a_buf[:, :, :rows].reshape(2 * C * rows, 128))
    pre1[...] = z1
    h1_buf[s] = silu(z1).astype(BF)
    z_bcast(h1_buf, H1)

    wait(qr_buf.at[pl.ds(0, S - 1)], recv.at[QKV])
    for j in range(S):
        x = qr_buf[j]
        q_scr[tok * j : tok * (j + 1)] = x[:tok, :DH]
        k_scr[tok * j : tok * (j + 1)] = x[:tok, DH:]
        v_scr[tok * j : tok * (j + 1)] = jnp.concatenate([x[tok:, :DH], x[tok:, DH:]], axis=0)

    inv_len = 1.0 / jnp.full((1, 1), length, jnp.int32).astype(F32)
    W = 256

    def attend(b):
        q = q_scr[W * b : W * (b + 1)]
        acc = jnp.zeros((W, DH), F32)
        for kb in range(b + 1):
            half = dot_t(q, k_scr[W * kb : W * (kb + 1)]) * (0.5 * DH ** (-0.5))
            w = (half * inv_len) * (1.0 + jnp.tanh(half))
            if kb == b:
                r = lax.broadcasted_iota(jnp.int32, (W, W), 0)
                cc = lax.broadcasted_iota(jnp.int32, (W, W), 1)
                w = jnp.where(cc <= r, w, 0.0)
            acc = acc + dot(w.astype(BF), v_scr[W * kb : W * (kb + 1)])
        pos = W * b + lax.broadcasted_iota(jnp.int32, (W, 1), 0)
        acc = jnp.where(pos < length, acc, 0.0).astype(BF)
        for i in range(W // tok):
            o = acc[tok * i : tok * (i + 1)]
            at_send[(W // tok) * b + i] = jnp.concatenate([o[: tok // 2], o[tok // 2 :]], axis=1)

    n_blocks = S * tok // W
    for b in range(n_blocks // 2, n_blocks):
        attend(b)

    wait(h1_buf.at[pl.ds(0, S - 1)], recv.at[H1])
    h1 = jnp.concatenate([h1_buf[j] for j in range(S)], axis=1)
    z2 = dot(h1, a_buf[:, :, rows:].reshape(2 * C * rows, 128))
    pre2[...] = z2
    h2_buf[s] = silu(z2).astype(BF)
    z_bcast(h2_buf, H2)

    for b in range(n_blocks // 2):
        attend(b)
    z_scatter(at_send, at_recv, ATT)
    at_recv[s] = at_send[s]

    wait(b_buf.at[pl.ds(0, C - 1), 0], recv.at[B])
    copy(b_buf.at[:, c], b_buf.at[:, c], BS, sib).start()

    wait(h2_buf.at[pl.ds(0, S - 1)], recv.at[H2])
    wait(b_buf.at[:, 0], recv.at[BS])
    h2 = jnp.concatenate([h2_buf[j] for j in range(S)], axis=1)
    raw = dot(h2, b_buf[...].reshape(2 * C * rows, 512))
    item_inverse = lax.rsqrt(jnp.sum(raw * raw, axis=-1, keepdims=True) + EPS_UNIT)
    unit_item = raw * item_inverse
    ui[...] = unit_item
    inv[...] = jnp.broadcast_to(item_inverse, inv.shape)
    pe_buf[p, c] = unit_item.astype(BF)

    copy(pe_buf.at[p, c], pe_buf.at[p, c], PES, sib).start()
    per = (C - 1) // 3

    def pe_step(k, _):
        t = lax.rem(p + k, C)
        grp = (k - 1) // per
        copy(pe_buf.at[p, c], pe_buf.at[p, c], 0, (s, 2 * t + c), PE + grp).start()
        return 0

    lax.fori_loop(1, C, pe_step, 0)

    wait(at_recv.at[pl.ds(0, S - 1)], recv.at[ATT])
    tops, bottoms = [], []
    for h in range(S):
        x = at_recv[h]
        tops.append(x[:, :DH])
        bottoms.append(x[:, DH:])
    merged = jnp.concatenate(
        [jnp.concatenate(tops, axis=1), jnp.concatenate(bottoms, axis=1)], axis=0).astype(F32)
    branch = (layer_norm(merged) * gate[...].astype(F32)).astype(BF)
    layer_out = (hist[...].astype(F32) + dot(branch, wout[...])).astype(BF)
    lo_ref[...] = layer_out
    outward = layer_out.astype(F32)
    user_inverse = lax.rsqrt(jnp.sum(outward * outward, axis=-1, keepdims=True) + EPS_UNIT)
    unit_user = outward * user_inverse
    unit_low = unit_user.astype(BF)
    uu[...] = unit_user
    uinv[...] = jnp.broadcast_to(user_inverse, uinv.shape)

    for j in range(3):
        wait(pe_buf.at[pl.ds(0, per), 0], recv.at[PE + j])

        def fwd(k, _):
            t = lax.rem(p + C - k, C)
            copy(pe_buf.at[t, c], pe_buf.at[t, c], PES, sib).start()
            return 0

        lax.fori_loop(1 + per * j, 1 + per * (j + 1), fwd, 0)

    eye = lax.broadcasted_iota(jnp.int32, (tok, tok), 0) == lax.broadcasted_iota(jnp.int32, (tok, tok), 1)
    items = jnp.sum(
        jnp.where(eye, jnp.broadcast_to(nxt[...].astype(F32), (tok, tok)), 0.0), axis=1, keepdims=True
    ).astype(jnp.int32)
    positions = s * tok + lax.broadcasted_iota(jnp.int32, (tok, 1), 0)
    valid = (positions < length - 1).astype(F32)

    wait(pe_buf.at[:, 0], recv.at[PES])

    Q = 4
    CQ = C // Q
    width = pe_buf.shape[0] * 2 * pe_buf.shape[2] // Q
    den = jnp.zeros((tok, 1), F32)
    positive = jnp.zeros((tok, 1), F32)
    for q in range(Q):
        rows_q = pe_buf[CQ * q : CQ * (q + 1)].reshape(width, 512)
        logit = TEMP * dot_t(unit_low, rows_q)
        r_id = width * q + lax.broadcasted_iota(jnp.int32, (tok, width), 1)
        own = r_id == items
        times = jnp.concatenate(
            [cnt[i : i + 1] for i in range(q * width // 128, (q + 1) * width // 128)], axis=1)
        e = jnp.where(own, 0.0, jnp.exp(logit) * times)
        em[q] = e
        den = den + jnp.sum(e, axis=1, keepdims=True)
        positive = positive + jnp.sum(jnp.where(own, logit, 0.0), axis=1, keepdims=True)
    positive_exp = jnp.exp(positive)
    den = den + positive_exp
    slope = valid * (positive_exp / den - 1.0)
    scale = valid / den
    loss_sum = jnp.sum(valid * (jnp.log(den) - positive))

    for q in range(Q):
        gq = lax.rem(p // CQ + q, Q)
        r_id = width * gq + lax.broadcasted_iota(jnp.int32, (tok, width), 1)
        sm = jnp.where(r_id == items, slope, scale * em[gq]).astype(BF)
        sl[gq] = sm
        term = (TEMP * t_dot(sm, unit_low)).astype(BF)
        pt_send[pl.ds(CQ * gq, CQ)] = term.reshape(CQ, 2, pe_buf.shape[2], 512)
        copy(pt_send.at[pl.ds(CQ * gq, CQ), 1 - c], pair_recv.at[pl.ds(CQ * gq, CQ)], 0, sib, PAIR + q).start()

    for q in range(Q):
        gq = lax.rem(p // CQ + q, Q)
        wait(pair_recv.at[pl.ds(CQ * gq, CQ)], recv.at[PAIR + q])
        both = pt_send[pl.ds(CQ * gq, CQ), c].astype(F32) + pair_recv[pl.ds(CQ * gq, CQ)].astype(F32)
        rs_send[pl.ds(CQ * gq, CQ)] = both.astype(BF)

        def rs_step(i, _):
            t = CQ * gq + lax.rem(p + i, CQ)

            @pl.when(t != p)
            def _():
                copy(rs_send.at[t], rs_recv.at[p], RS, (s, 2 * t + c)).start()
            return 0

        lax.fori_loop(0, CQ, rs_step, 0)

    user_dir = jnp.zeros((tok, 512), F32)
    for q in range(Q):
        user_dir = user_dir + dot(sl[q], pe_buf[CQ * q : CQ * (q + 1)].reshape(width, 512))
    user_dir = TEMP * user_dir
    uun = uu[...]
    ug_ref[...] = uinv[:, :1] * (user_dir - uun * jnp.sum(uun * user_dir, axis=-1, keepdims=True))

    wait(rs_recv.at[pl.ds(0, C - 1)], recv.at[RS])
    rs_recv[p] = rs_send[p]
    part = jnp.sum(rs_recv[...].astype(F32), axis=0)
    lane = lax.broadcasted_iota(jnp.int32, (8, 128), 1)
    count = jnp.full((8, 128), length - 1, jnp.int32).astype(F32)
    tail = jnp.where(lane == 0, loss_sum, jnp.where(lane == 1, count, 0.0))
    for t in range(S):
        zs_send[t, :, :512] = part[8 * t : 8 * (t + 1)]
        zs_send[t, :, 512:] = tail
    z_scatter(zs_send, zs_recv, ZR)
    wait(zs_recv.at[pl.ds(0, S - 1)], recv.at[ZR])
    zs_recv[s] = zs_send[s]
    total = zs_recv[0]
    for t in range(1, S):
        total = total + zs_recv[t]
    own_grad = total[:, :512]
    own_rows = pl.ds(pl.multiple_of(s * 8, 8), 8)
    ui8 = ui[own_rows]
    raw8 = inv[own_rows][:, :1] * (own_grad - ui8 * jnp.sum(ui8 * own_grad, axis=-1, keepdims=True))
    zg_buf[s] = raw8.astype(BF).astype(F32)
    z_bcast(zg_buf, ZG)
    loss_row = total[0:1, 512:]
    loss_hi = loss_row.astype(BF).astype(F32)
    loss_lo = loss_row - loss_hi
    row16 = lax.broadcasted_iota(jnp.int32, (16, 128), 0)
    loss16 = jnp.where(row16 == 0, loss_hi, jnp.where(row16 == 1, loss_lo, 0.0)).astype(BF)
    wait(zg_buf.at[pl.ds(0, S - 1)], recv.at[ZG])
    raw_grad = zg_buf[...].reshape(8 * S, 512).astype(BF)
    rg[...] = raw_grad

    w3_rows = b_buf[pl.ds(128 // (2 * rows) * s, 128 // (2 * rows))].reshape(128, 512)
    sg = (dot_t(raw_grad, w3_rows) * silu_slope(pre2[...])).astype(BF)
    back = dot_t(sg, a_buf[:, :, rows:].reshape(2 * C * rows, 128)).astype(BF)
    for t in range(S):
        p_send[t] = back[:, 128 * t : 128 * (t + 1)]
    z_scatter(p_send, p_recv, PP)
    p_recv[s] = p_send[s]

    h1 = jnp.concatenate([h1_buf[j] for j in range(S)], axis=1)
    h2 = jnp.concatenate([h2_buf[j] for j in range(S)], axis=1)
    q_cols = pl.ds(pl.multiple_of(lax.rem(s, 4) * 128, 128), 128)
    half = rows // 2
    gl_scr[...] = t_dot(h2, rg[:, q_cols]).astype(BF).reshape(G, 2, half, 128)
    g1_send[:, :rows] = t_dot(h1, sg).astype(BF).reshape(G, rows, 128)
    g1_send[:, rows : rows + half] = gl_scr[:, s // 4]
    g1_send[:, rows + half :] = jnp.broadcast_to(loss16[None], (G, 16, 128))
    grp_scatter(g1_send, g1_recv, G1)
    g1_recv[g] = g1_send[g]

    wait(p_recv.at[pl.ds(0, S - 1)], recv.at[PP])
    back1 = p_recv[0].astype(F32)
    for t in range(1, S):
        back1 = back1 + p_recv[t].astype(F32)
    fg = (back1 * silu_slope(pre1[...])).astype(BF)
    g2_send[...] = t_dot(xf[...], fg).astype(BF).reshape(G, rows, 128)
    grp_scatter(g2_send, g2_recv, G2)
    g2_recv[g] = g2_send[g]

    wait(g1_recv.at[pl.ds(0, G - 1)], recv.at[G1])
    sum1 = jnp.sum(g1_recv[...].astype(F32), axis=0)
    f1_buf[s] = sum1[: rows + half].astype(BF)
    z_bcast(f1_buf, F1)
    both = sum1[rows + half : rows + half + 1] + sum1[rows + half + 1 : rows + half + 2]
    lane1 = lax.broadcasted_iota(jnp.int32, (1, 128), 1)
    numer = jnp.sum(jnp.where(lane1 == 0, both, 0.0), axis=1, keepdims=True)
    denom = jnp.sum(jnp.where(lane1 == 1, both, 0.0), axis=1, keepdims=True)
    loss_ref[...] = jnp.broadcast_to(numer * S / denom, loss_ref.shape)

    wait(g2_recv.at[pl.ds(0, G - 1)], recv.at[G2])
    f2_buf[s] = jnp.sum(g2_recv[...].astype(F32), axis=0).astype(BF)
    z_bcast(f2_buf, F2)

    wait(f1_buf.at[pl.ds(0, S - 1)], recv.at[F1])
    for t in range(S):
        gm_ref[:, 128 * t : 128 * (t + 1)] = f1_buf[t, :rows].astype(F32)
        gl_ref[half * (t // 4) : half * (t // 4 + 1), 128 * (t % 4) : 128 * (t % 4 + 1)] = f1_buf[t, rows:].astype(F32)

    wait(a_buf.at[pl.ds(0, C - 1), 0], send.at[A])
    wait(b_buf.at[pl.ds(0, C - 1), 0], send.at[B])
    wait(a_buf.at[:, 0], send.at[AS])
    wait(b_buf.at[:, 0], send.at[BS])
    wait(pe_buf.at[:, 0], send.at[PES])
    for j in range(3):
        wait(pe_buf.at[pl.ds(0, per), 0], send.at[PE + j])
    for q in range(Q):
        wait(pair_recv.at[pl.ds(0, CQ)], send.at[PAIR + q])
    wait(rs_recv.at[pl.ds(0, C - 1)], send.at[RS])
    for buf, i in ((qr_buf, QKV), (at_recv, ATT), (h1_buf, H1), (h2_buf, H2), (zs_recv, ZR), (zg_buf, ZG),
                   (p_recv, PP), (f1_buf, F1)):
        wait(buf.at[pl.ds(0, S - 1)], send.at[i])
    wait(g1_recv.at[pl.ds(0, G - 1)], send.at[G1])
    wait(g2_recv.at[pl.ds(0, G - 1)], send.at[G2])

    wait(f2_buf.at[pl.ds(0, S - 1)], recv.at[F2])
    for t in range(S):
        gf_ref[:, 128 * t : 128 * (t + 1)] = f2_buf[t].astype(F32)
    wait(f2_buf.at[pl.ds(0, S - 1)], send.at[F2])


def local(history, lengths, next_items, negatives, input_weight, output_weight, pool_features,
          tower_first, tower_middle, tower_last, S, G):
    events = history[0]
    tok = events.shape[0]
    C = G // 2
    R = pool_features.shape[0]
    rows = tower_first.shape[0]
    V = pltpu.VMEM
    vmem = pl.BlockSpec(memory_space=pltpu.VMEM)
    width = 2 * C * R // 4
    scratch = [
        pltpu.SemaphoreType.DMA((N_SEM,)),
        pltpu.SemaphoreType.DMA((N_SEM,)),
        V((C, 2, 2 * rows, 128), BF),
        V((C, 2, rows, 512), BF),
        V((S, tok + tok // 2, 128), BF),
        V((S, tok + tok // 2, 128), BF),
        V((tok, 512), BF),
        V((S * tok, DH), BF),
        V((S * tok, DH), BF),
        V((S * tok, DH), BF),
        V((S, tok // 2, 128), BF),
        V((S, tok // 2, 128), BF),
        V((S, R, 128), BF),
        V((S, R, 128), BF),
        V((R, 128), F32),
        V((R, 128), F32),
        V((R, 512), F32),
        V((R, 128), F32),
        V((C, 2, R, 512), BF),
        V((4, tok, width), F32),
        V((4, tok, width), BF),
        V((C, 2, R, 512), BF),
        V((C, R, 512), BF),
        V((C, R, 512), BF),
        V((C, R, 512), BF),
        V((S, 8, 640), F32),
        V((S, 8, 640), F32),
        V((S, 8, 512), F32),
        V((R, 512), BF),
        V((S, R, 128), BF),
        V((S, R, 128), BF),
        V((G, 2, rows // 2, 128), BF),
        V((G, rows + rows // 2 + 16, 128), BF),
        V((G, rows + rows // 2 + 16, 128), BF),
        V((G, rows, 128), BF),
        V((G, rows, 128), BF),
        V((S, rows + rows // 2, 128), BF),
        V((S, rows, 128), BF),
        V((2 * C * R // 128, 128), F32),
        V((tok, 512), F32),
        V((tok, 128), F32),
    ]
    lo, loss, ug, gf, gm, gl = pl.pallas_call(
        functools.partial(kernel, S, G),
        out_shape=[
            jax.ShapeDtypeStruct((tok, 512), BF),
            jax.ShapeDtypeStruct((8, 128), F32),
            jax.ShapeDtypeStruct((tok, 512), F32),
            jax.ShapeDtypeStruct((rows, 1024), F32),
            jax.ShapeDtypeStruct((rows, 1024), F32),
            jax.ShapeDtypeStruct((rows, 512), F32),
        ],
        in_specs=[pl.BlockSpec(memory_space=pltpu.SMEM)] + [vmem] * 9,
        out_specs=[vmem] * 6,
        scratch_shapes=scratch,
        compiler_params=pltpu.CompilerParams(
            collective_id=0, has_side_effects=True, vmem_limit_bytes=48 * 1024 * 1024),
    )(lengths, events, next_items, negatives, input_weight, output_weight, pool_features,
      tower_first, tower_middle, tower_last)
    return lo[None], loss[0, 0], ug[None], gf, gm, gl


def solution(mesh):
    placed = (
        P("grp", "seq", None), P("grp"), P("grp", "seq"), P("grp", None), P(), P(),
        P("grp", None), P("grp", None), P("grp", None), P("grp", None),
    )
    return jax.shard_map(
        functools.partial(local, S=mesh.shape["seq"], G=mesh.shape["grp"]),
        mesh=mesh,
        in_specs=placed,
        out_specs=(
            P("grp", "seq", None), P(), P("grp", "seq", None),
            P("grp", None), P("grp", None), P("grp", None),
        ),
        check_vma=False,
    )
```

time: 686 us -> 110 us (0.16)
  waiting for transfers between devices: 503 us -> 0 us
  Pallas kernels: 0 us -> 96.2 us
  blocking collectives: 80.1 us -> 0 us
  other arithmetic: 24.4 us -> 0 us
  matrix products: 24.1 us -> 0 us
  starting transfers between devices: 16.1 us -> 0 us
  between operations: 17.3 us -> 1.31 us
  local copies, waits for them, and re-layouts: 19.3 us -> 12 us
    reduce_scatter x3 -> x0, waiting for transfers between devices: 181 us -> none  [the longest x2 94 us: outer_sum(): lax.psum_scatter(lax.dot_general(left, right, (((0,), (0,)), ((), ())), p...]
    all_gather x4 -> x0, waiting for transfers between devices: 145 us -> none  [the longest x1 48.6 us: local(): lax.all_gather(tower_middle, 'grp', axis=0, tiled=True)]
    pallas_call x0 -> x1, Pallas kernels: none -> 96.2 us  [local(): pl.pallas_call(functools.partial(kernel, S, G), out_shape=[jax.ShapeDtype...]
    unnamed x10 -> x0, waiting for transfers between devices: 87 us -> none
    psum x1 -> x0, blocking collectives: 80.1 us -> none  [local(): loss_parts = lax.psum((loss_sum, count_term), ('seq', 'grp'))]
    psum x1 -> x0, waiting for transfers between devices: 70.2 us -> none  [local(): own_grad = lax.psum(owned_part, 'seq')]
    dot_general x13 -> x0, matrix products: 24.1 us -> none  [the longest x3 9.43 us: outer_sum(): lax.dot_general(left, right, (((0,), (0,)), ((), ())), preferred_element_...]
    all_to_all x2 -> x0, waiting for transfers between devices: 19.7 us -> none  [the longest x1 12.9 us: local(): lax.all_to_all(mixed_heads, 'seq', split_axis=1, concat_axis=0, tiled=True)]
  transfers between devices with their start and end apart: 11 -> 0, of which waited for: 10 -> 0; matrix products, arithmetic and copies ran while one was open for 5% -> 0% of each run, Pallas kernels for 0% -> 0%
where the time goes in v1:
time: 110 us
  Pallas kernels  96.2 us (87%)
  local copies, waits for them, and re-layouts  12 us (11%)
  between operations  1.31 us (1%)
    pallas_call x1, Pallas kernels, local(): pl.pallas_call(functools.partial(kernel, S, G), out_shape=[jax.ShapeDtype...  96.2 us
    unnamed x23, local copies, waits for them, and re-layouts  11.5 us

profile of v1, /device:TPU:1, one launch (start us, length us, event | category | flops | bytes accessed | tf_op | source)
XLA Modules:
  0.0 109.6 jit_solution(2889446291998538726)
XLA Ops:
  1.3 0.0 copy-start
  1.3 1.6 %copy-done = bf16[512,2048]{1,0:T(8,128)(2,1)S(1)} copy-done((bf16[512,2048]{1,0:T(8,128)(2,1)S(1)}, bf16[512,2048]{1,0:T(8,128)(2,1)}, u32[]{:S(2)}) %copy-start) | copy-done | bytes 2097176
  2.9 0.0 copy-start.1
  2.9 1.0 copy-done.1
  3.9 0.0 copy-start.2
  3.9 0.9 copy-done.2
  4.8 0.0 copy-start.3
  4.8 0.9 copy-done.3
  5.7 0.0 copy-start.4
  5.7 0.8 copy-done.4
  6.6 0.0 copy-start.5
  6.6 0.8 copy-done.5
  7.4 0.0 copy-start.6
  7.4 0.8 copy-done.6
  8.2 0.0 copy-start.7
  8.2 0.7 copy-done.7
  8.8 0.0 copy-start.8
  8.8 0.7 copy-done.8
  9.5 96.2 %shard_map.145 = (bf16[128,512]{1,0:T(8,128)(2,1)S(1)}, f32[8,128]{1,0:T(8,128)S(1)}, f32[128,512]{1,0:T(8,128)S(1)}, f32[32,1024]{1,0:T(8,128)S(1)}, f32[32,1024]{1,0:T(8,128)S(1)}, /*index=5*/f32[32,512]{1,0:T(8,128)S(1)}) custom-call(s32[1]{0:T(128)S(6)} %copy.21.len_ref, bf16[128,512]{1,0:T(8,128)(2,1)S(1)} %bitcast.5, s32[1,128]{1,0:T(1,128)S(1)} %copy-done.8, ...), custom_call_target="tpu_custom_call" | custom-call | tf_op jit(solution)/shard_map/pallas_call | solution.py:476
  105.7 0.5 slice.3
  106.3 0.7 copy.22
  106.9 0.7 copy.23
  107.6 0.7 copy.24
  108.3 0.7 copy.25
  108.9 0.6 copy.26
Async XLA Ops:
  1.3 1.6 %copy-start = (bf16[512,2048]{1,0:T(8,128)(2,1)S(1)}, bf16[512,2048]{1,0:T(8,128)(2,1)}, u32[]{:S(2)}) copy-start(bf16[512,2048]{1,0:T(8,128)(2,1)} %win.1) | copy-start | bytes 6291460
  2.9 1.0 copy-start.1
  3.9 0.9 copy-start.2
  4.8 0.9 copy-start.3
  5.7 0.8 copy-start.4
  6.6 0.8 copy-start.5
  7.4 0.8 copy-start.6
  8.2 0.7 copy-start.7
  8.8 0.7 copy-start.8

commit v2 on v1

v2 whole, which is shorter than its diff:
```python
import functools

import jax
import jax.numpy as jnp
from jax import lax
from jax.experimental import pallas as pl
from jax.experimental.pallas import tpu as pltpu
from jax.sharding import PartitionSpec as P

DH = 64
EPS_NORM = 1e-05
EPS_UNIT = 1e-06
TEMP = 20.0

MESH = pl.DeviceIdType.MESH
BF = jnp.bfloat16
F32 = jnp.float32

(A, A2, B, AS, AS2, BS, QKV, ATT, H1, H2, SL2, PES, HX, NX, DN, UD, ZA, ZL, GL, G1, G2, F1, F2, RS, W2, W2S) = range(26)
PE, PAIR = 26, 29
N_SEM = 34

(I_W3, I_H, I_WIN, I_WOUT, I_X, I_NEG, I_NXT, I_W2R, O_LO, O_UG) = range(10)
I_W1, I_W2 = 10, 11
N_HERE = 15


def silu(x):
    half = 0.5 * x
    return half * (1.0 + jnp.tanh(half))


def silu_slope(z):
    sigma = 0.5 * (1.0 + jnp.tanh(0.5 * z))
    return sigma * (1.0 + z * (1.0 - sigma))


def layer_norm(values):
    center = values - jnp.mean(values, axis=-1, keepdims=True)
    spread = jnp.mean(center * center, axis=-1, keepdims=True)
    return center * lax.rsqrt(spread + EPS_NORM)


def dot(a, b):
    return jnp.dot(a, b, preferred_element_type=F32)


def dot_t(a, b):
    return lax.dot_general(a, b, (((1,), (1,)), ((), ())), preferred_element_type=F32)


def t_dot(a, b):
    return lax.dot_general(a, b, (((0,), (0,)), ((), ())), preferred_element_type=F32)


def wait(ref, sem):
    pltpu.make_async_copy(ref, ref, sem).wait()


def kernel(
    S, G,
    len_ref, hist, nxt, neg, win, wout, xf, w1, w2, w3,
    lo_ref, loss_ref, ug_ref, gf_ref, gm_ref, gl_ref,
    send, recv, here,
    h256, nx_buf, neg_v, win_v, wout_v, xf_v,
    a_buf, a2_buf, b_buf, w2r_buf, qs_buf, qr_buf, gate, k_scr, q_scr, v_scr, at_send, at_recv,
    h1_buf, h2_buf, sl2_buf, pre1, ui, inv, pe_buf, em, st, pt_send, pair_recv, rs_send, rs_recv,
    dn_send, dn_recv, ud, ud_send, ud_recv, lo_scr, zl_buf, lg_buf, za_buf, rg, sg_scr,
    gl_scr, g1_send, g1_recv, g2_send, g2_recv, f1_buf, f2_buf, cnt, uu, uinv,
):
    C = G // 2
    s = lax.axis_index("seq")
    g = lax.axis_index("grp")
    p = g // 2
    c = g % 2
    par = s % 2
    tok = h256.shape[1]
    rows = b_buf.shape[2]
    NB = a2_buf.shape[2]
    half = rows // 2
    R = xf_v.shape[0]
    RH = R // 2
    length = len_ref[0]
    pair = (s + 1 - 2 * par, g)
    sib = (s, 2 * p + 1 - c)
    cols = pl.ds(pl.multiple_of(s * 128, 128), 128)

    def copy(src, dst, i, dev):
        return pltpu.make_async_remote_copy(
            src_ref=src, dst_ref=dst, send_sem=send.at[i], recv_sem=recv.at[i],
            device_id=dev, device_id_type=MESH)

    def fetch(src, dst, i):
        pltpu.make_async_copy(src, dst, here.at[i]).start()

    def z_bcast(buf, i):
        def step(k, _):
            copy(buf.at[s], buf.at[s], i, (lax.rem(s + k, S), g)).start()
            return 0
        lax.fori_loop(1, S, step, 0)

    def chips(src, dst, i):
        def step(k, _):
            copy(src, dst, i, (s, 2 * lax.rem(p + k, C) + c)).start()
            return 0
        lax.fori_loop(1, C, step, 0)

    def grp_scatter(src, dst, i):
        def step(k, _):
            t = lax.rem(g + k, G)
            copy(src.at[t], dst.at[g], i, (s, t)).start()
            return 0
        lax.fori_loop(1, G, step, 0)

    barrier = pltpu.get_barrier_semaphore()

    def greet_grp(k, _):
        pl.semaphore_signal(barrier, inc=1, device_id=(s, lax.rem(g + k, G)), device_id_type=MESH)
        return 0

    def greet_seq(k, _):
        pl.semaphore_signal(barrier, inc=1, device_id=(lax.rem(s + k, S), g), device_id_type=MESH)
        return 0

    lax.fori_loop(1, G, greet_grp, 0)
    lax.fori_loop(1, S, greet_seq, 0)

    fetch(hist, h256.at[par], I_H)
    fetch(w1.at[:, cols], a_buf.at[p, c], I_W1)
    for j in range(NB):
        block = pl.ds(pl.multiple_of((2 * j + par) * 128, 128), 128)
        fetch(w2.at[:, block], a2_buf.at[p, c, j], I_W2 + j)
    fetch(win, win_v, I_WIN)
    fetch(nxt, nx_buf.at[par], I_NXT)
    fetch(w3, b_buf.at[p, c], I_W3)
    fetch(xf, xf_v, I_X)
    fetch(neg, neg_v, I_NEG)
    fetch(wout, wout_v, I_WOUT)
    source = p // 2 == s

    @pl.when(source)
    def _():
        fetch(w2, w2r_buf.at[p % 2, c], I_W2R)

    wait(h256.at[par], here.at[I_H])
    normed = layer_norm(h256[par].astype(F32)).astype(BF)
    wait(win_v, here.at[I_WIN])
    for j in range(4):
        x = silu(dot(normed, win_v[:, 512 + 384 * j : 512 + 384 * (j + 1)])).astype(BF)
        for e in (0, 1):
            o = 192 * e
            qs_buf[2 * j + e, :tok] = x[:, o : o + 128]
            v = x[:, o + 128 : o + 192]
            qs_buf[2 * j + e, tok:] = jnp.concatenate([v[: tok // 2], v[tok // 2 :]], axis=1)
    wait(a_buf.at[p, c], here.at[I_W1])
    for j in range(NB):
        wait(a2_buf.at[p, c, j], here.at[I_W2 + j])
    wait(nx_buf.at[par], here.at[I_NXT])
    wait(b_buf.at[p, c], here.at[I_W3])
    pl.semaphore_wait(barrier, (G - 1) + (S - 1))

    chips(a_buf.at[p, c], a_buf.at[p, c], A)

    def qkv_step(k, _):
        t = lax.rem(s + k, S)
        copy(qs_buf.at[t], qr_buf.at[s], QKV, (t, g)).start()
        return 0

    lax.fori_loop(1, S, qkv_step, 0)
    qr_buf[s] = qs_buf[s]

    def local_row(ids):
        mine = (ids // RH) % 2 == par
        return jnp.where(mine, (ids // R) * RH + ids % RH, -1)

    wait(neg_v, here.at[I_NEG])
    n_rows = G * RH
    ids = local_row(neg_v[...])
    hot = (lax.broadcasted_iota(jnp.int32, (n_rows, ids.shape[1]), 0) == ids).astype(F32).astype(BF)
    cnt[...] = dot(hot, jnp.ones((ids.shape[1], 128), BF))

    chips(a2_buf.at[p, c], a2_buf.at[p, c], A2)
    wait(xf_v, here.at[I_X])
    wait(a_buf.at[pl.ds(0, C - 1), 0], recv.at[A])
    copy(a_buf.at[:, c], a_buf.at[:, c], AS, sib).start()
    wait(a_buf.at[:, 0], recv.at[AS])
    z1 = dot(xf_v[...], a_buf[...].reshape(G * rows, 128))
    pre1[...] = z1
    h1_buf[s] = silu(z1).astype(BF)
    z_bcast(h1_buf, H1)
    def whole(buf):
        return jnp.concatenate([buf[j % 2, j // 2] for j in range(2 * NB)], axis=1)

    wait(a2_buf.at[pl.ds(0, C - 1), 0], recv.at[A2])
    copy(a2_buf.at[:, c], a2_buf.at[:, c], AS2, sib).start()
    chips(b_buf.at[p, c], b_buf.at[p, c], B)
    wait(qr_buf.at[pl.ds(0, S - 1)], recv.at[QKV])
    copy(h256.at[par], h256.at[par], HX, pair).start()
    copy(nx_buf.at[par], nx_buf.at[par], NX, pair).start()
    for j in range(S):
        x = qr_buf[j]
        q_scr[tok * j : tok * (j + 1)] = x[:tok, :DH]
        k_scr[tok * j : tok * (j + 1)] = x[:tok, DH:]
        v_scr[tok * j : tok * (j + 1)] = jnp.concatenate([x[tok:, :DH], x[tok:, DH:]], axis=0)

    inv_len = 1.0 / jnp.full((1, 1), length, jnp.int32).astype(F32)
    W = 2 * tok

    def attend(b):
        q = q_scr[W * b : W * (b + 1)]
        acc = jnp.zeros((W, DH), F32)
        for kb in range(b + 1):
            hs = dot_t(q, k_scr[W * kb : W * (kb + 1)]) * (0.5 * DH ** (-0.5))
            w = (hs * inv_len) * (1.0 + jnp.tanh(hs))
            if kb == b:
                r = lax.broadcasted_iota(jnp.int32, (W, W), 0)
                cc = lax.broadcasted_iota(jnp.int32, (W, W), 1)
                w = jnp.where(cc <= r, w, 0.0)
            acc = acc + dot(w.astype(BF), v_scr[W * kb : W * (kb + 1)])
        pos = W * b + lax.broadcasted_iota(jnp.int32, (W, 1), 0)
        acc = jnp.where(pos < length, acc, 0.0).astype(BF)
        at_send[b] = jnp.concatenate([acc[:tok], acc[tok:]], axis=1)

    for b in reversed(range(S // 2)):
        attend(b)
    at_recv[s] = at_send[s // 2]

    wait(h1_buf.at[pl.ds(0, S - 1)], recv.at[H1])
    wait(a2_buf.at[:, 0], recv.at[AS2])
    h1 = jnp.concatenate([h1_buf[j] for j in range(S)], axis=1)
    for j in range(NB):
        z2 = dot(h1, a2_buf[:, :, j].reshape(G * rows, 128))
        h2_buf[par, j] = silu(z2).astype(BF)
        sl2_buf[par, j] = silu_slope(z2).astype(BF)
    copy(h2_buf.at[par], h2_buf.at[par], H2, pair).start()

    def at_step(k, _):
        t = lax.rem(s + k, S)
        copy(at_send.at[t // 2], at_recv.at[s], ATT, (t, g)).start()
        return 0

    lax.fori_loop(1, S, at_step, 0)
    wait(h256.at[0], recv.at[HX])
    copy(sl2_buf.at[par], sl2_buf.at[par], SL2, pair).start()
    both = h256[...].reshape(2 * tok, 512)
    gate[...] = silu(dot(layer_norm(both.astype(F32)).astype(BF), win_v[:, :512])).astype(BF)

    wait(b_buf.at[pl.ds(0, C - 1), 0], recv.at[B])
    copy(b_buf.at[:, c], b_buf.at[:, c], BS, sib).start()

    wait(h2_buf.at[0], recv.at[H2])
    wait(b_buf.at[:, 0], recv.at[BS])
    h2 = whole(h2_buf)
    raw = dot(h2, b_buf[...].reshape(G * rows, 512))
    item_inverse = lax.rsqrt(jnp.sum(raw * raw, axis=-1, keepdims=True) + EPS_UNIT)
    unit_item = raw * item_inverse
    ui[...] = unit_item
    inv[...] = jnp.broadcast_to(item_inverse, inv.shape)
    pe_buf[p, c] = ui[pl.ds(pl.multiple_of(par * RH, RH), RH)].astype(BF)

    copy(pe_buf.at[p, c], pe_buf.at[p, c], PES, sib).start()
    per = (C - 1) // 3

    def pe_step(k, _):
        t = lax.rem(p + k, C)
        copy(pe_buf.at[p, c], pe_buf.at[p, c], PE + (k - 1) // per, (s, 2 * t + c)).start()
        return 0

    lax.fori_loop(1, C, pe_step, 0)

    @pl.when(source)
    def _():
        wait(w2r_buf.at[p % 2, c], here.at[I_W2R])
        chips(w2r_buf.at[p % 2, c], w2r_buf.at[p % 2, c], W2)

    wait(wout_v, here.at[I_WOUT])
    wait(at_recv.at[pl.ds(0, S - 1)], recv.at[ATT])
    tops, bottoms = [], []
    for h in range(S):
        x = at_recv[h]
        tops.append(x[:, :DH])
        bottoms.append(x[:, DH:])
    merged = jnp.concatenate(
        [jnp.concatenate(tops, axis=1), jnp.concatenate(bottoms, axis=1)], axis=0).astype(F32)
    branch = (layer_norm(merged) * gate[...].astype(F32)).astype(BF)
    layer_out = (h256[...].reshape(2 * tok, 512).astype(F32) + dot(branch, wout_v[...])).astype(BF)
    lo_scr[...] = layer_out.reshape(2, tok, 512)
    pltpu.make_async_copy(lo_scr.at[par], lo_ref, here.at[O_LO]).start()
    outward = layer_out.astype(F32)
    user_inverse = lax.rsqrt(jnp.sum(outward * outward, axis=-1, keepdims=True) + EPS_UNIT)
    unit_user = outward * user_inverse
    unit_low = unit_user.astype(BF)
    uu[...] = unit_user.reshape(2, tok, 512)
    uinv[...] = jnp.broadcast_to(user_inverse, (2 * tok, 128)).reshape(2, tok, 128)

    wait(nx_buf.at[0], recv.at[NX])
    items = local_row(jnp.concatenate([nx_buf[0], nx_buf[1]], axis=1))
    pair_pos = lax.broadcasted_iota(jnp.int32, (1, W), 1)
    positions = (s // 2) * W + pair_pos
    valid = (positions < length - 1).astype(F32)

    for j in range(3):
        wait(pe_buf.at[pl.ds(0, per), 0], recv.at[PE + j])

        def fwd(k, _):
            t = lax.rem(p + C - k, C)
            copy(pe_buf.at[t, c], pe_buf.at[t, c], PES, sib).start()
            return 0

        lax.fori_loop(1 + per * j, 1 + per * (j + 1), fwd, 0)

    wait(pe_buf.at[:, 0], recv.at[PES])

    Q = 4
    CQ = C // Q
    width = n_rows // Q
    row_id = lax.broadcasted_iota(jnp.int32, (width, W), 0)
    den = jnp.zeros((1, W), F32)
    positive = jnp.zeros((1, W), F32)
    for q in range(Q):
        logit = TEMP * dot_t(pe_buf[CQ * q : CQ * (q + 1)].reshape(width, 512), unit_low)
        own = row_id + width * q == items
        times = cnt[width * q : width * (q + 1)]
        e = jnp.where(own, 0.0, jnp.exp(logit) * jnp.concatenate([times] * (W // 128), axis=1))
        em[q] = e
        den = den + jnp.sum(e, axis=0, keepdims=True)
        positive = positive + jnp.sum(jnp.where(own, logit, 0.0), axis=0, keepdims=True)
    row8 = lax.broadcasted_iota(jnp.int32, (8, W), 0)
    dn_send[...] = jnp.where(row8 == 0, den, positive)
    copy(dn_send, dn_recv, DN, pair).start()
    wait(dn_recv, recv.at[DN])
    den = den + dn_recv[0:1]
    positive = positive + dn_recv[1:2]
    positive_exp = jnp.exp(positive)
    den = den + positive_exp
    slope = valid * (positive_exp / den - 1.0)
    scale = valid / den

    for q in range(Q):
        gq = lax.rem(p // CQ + q, Q)
        sm = jnp.where(row_id + width * gq == items, slope, scale * em[gq]).astype(BF)
        st[gq] = sm
        pt_send[pl.ds(CQ * gq, CQ)] = (TEMP * dot(sm, unit_low)).astype(BF).reshape(CQ, 2, RH, 512)
        copy(pt_send.at[pl.ds(CQ * gq, CQ), 1 - c], pair_recv.at[pl.ds(CQ * gq, CQ)], PAIR + q, sib).start()

    for q in range(Q):
        gq = lax.rem(p // CQ + q, Q)
        wait(pair_recv.at[pl.ds(CQ * gq, CQ)], recv.at[PAIR + q])
        chip_sum = pt_send[pl.ds(CQ * gq, CQ), c].astype(F32) + pair_recv[pl.ds(CQ * gq, CQ)].astype(F32)
        rs_send[pl.ds(CQ * gq, CQ)] = chip_sum.astype(BF)

        def rs_step(i, _):
            t = CQ * gq + lax.rem(p + i, CQ)

            @pl.when(t != p)
            def _():
                copy(rs_send.at[t], rs_recv.at[p], RS, (s, 2 * t + c)).start()
            return 0

        lax.fori_loop(0, CQ, rs_step, 0)

    mine = pair_pos // tok == par
    loss_sum = jnp.sum(jnp.where(mine, valid * (jnp.log(den) - positive), 0.0))
    lane = lax.broadcasted_iota(jnp.int32, (8, 128), 1)
    count = jnp.full((8, 128), length - 1, jnp.int32).astype(F32)
    zl_buf[s] = jnp.where(lane == 0, loss_sum, jnp.where(lane == 1, count, 0.0))
    z_bcast(zl_buf, ZL)

    user_dir = t_dot(st[...].reshape(n_rows, W), pe_buf[...].reshape(n_rows, 512))
    ud[...] = user_dir.reshape(2, tok, 512)
    ud_send[...] = ud[1 - par].astype(BF)
    copy(ud_send, ud_recv, UD, pair).start()

    @pl.when(source)
    def _():
        wait(w2r_buf.at[0, 0], recv.at[W2])

    @pl.when(jnp.logical_not(source))
    def _():
        wait(w2r_buf.at[:, 0], recv.at[W2])

    copy(w2r_buf.at[:, c], w2r_buf.at[:, c], W2S, sib).start()

    wait(rs_recv.at[pl.ds(0, C - 1)], recv.at[RS])
    rs_recv[p] = rs_send[p]
    za_buf[s] = jnp.sum(rs_recv[...].astype(F32), axis=0).astype(BF)
    z_bcast(za_buf, ZA)

    wait(zl_buf.at[pl.ds(0, S - 1)], recv.at[ZL])
    lg_buf[g] = jnp.sum(zl_buf[...], axis=0)

    def lg_step(k, _):
        copy(lg_buf.at[g], lg_buf.at[g], GL, (s, lax.rem(g + k, G))).start()
        return 0

    lax.fori_loop(1, G, lg_step, 0)
    wait(ud_recv, recv.at[UD])
    user_dir = TEMP * (ud[par] + ud_recv[...].astype(F32))
    uun = uu[par]
    ud[par] = uinv[par][:, :1] * (user_dir - uun * jnp.sum(uun * user_dir, axis=-1, keepdims=True))
    pltpu.make_async_copy(ud.at[par], ug_ref, here.at[O_UG]).start()
    wait(w2r_buf.at[:, 0], recv.at[W2S])
    wait(sl2_buf.at[0], recv.at[SL2])
    h1 = jnp.concatenate([h1_buf[j] for j in range(S)], axis=1)
    h2 = whole(h2_buf)
    slope2 = whole(sl2_buf).astype(F32)
    slope1 = silu_slope(pre1[...])

    wait(za_buf.at[pl.ds(0, S - 1)], recv.at[ZA])
    sums = []
    for e in (0, 1):
        part = za_buf[e].astype(F32)
        for t in range(e + 2, S, 2):
            part = part + za_buf[t].astype(F32)
        sums.append(part)
    own_grad = jnp.concatenate(sums, axis=0)
    uin = ui[...]
    raw_grad = (inv[:, :1] * (own_grad - uin * jnp.sum(uin * own_grad, axis=-1, keepdims=True))).astype(BF)
    rg[...] = raw_grad
    sg = (dot_t(raw_grad, b_buf[...].reshape(G * rows, 512)) * slope2).astype(BF)
    sg_scr[...] = sg
    fg = (dot_t(sg, w2r_buf[...].reshape(4 * rows, 1024)) * slope1).astype(BF)
    g2_send[...] = t_dot(xf_v[...], fg).astype(BF).reshape(G, rows, 128)
    grp_scatter(g2_send, g2_recv, G2)
    g2_recv[g] = g2_send[g]
    q_cols = pl.ds(pl.multiple_of(lax.rem(s, 4) * 128, 128), 128)
    gl_scr[...] = t_dot(h2, rg[:, q_cols]).astype(BF).reshape(G, 2, half, 128)
    g1_send[:, :rows] = t_dot(h1, sg_scr[:, cols]).astype(BF).reshape(G, rows, 128)
    g1_send[:, rows:] = gl_scr[:, s // 4]
    grp_scatter(g1_send, g1_recv, G1)
    g1_recv[g] = g1_send[g]

    wait(lg_buf.at[pl.ds(0, G - 1)], recv.at[GL])
    total = jnp.sum(lg_buf[...], axis=0)
    numer = jnp.sum(jnp.where(lane == 0, total, 0.0), axis=1, keepdims=True)
    denom = jnp.sum(jnp.where(lane == 1, total, 0.0), axis=1, keepdims=True)
    loss_ref[...] = jnp.broadcast_to(numer * S / denom, loss_ref.shape)

    wait(g2_recv.at[pl.ds(0, G - 1)], recv.at[G2])
    f2_buf[s] = jnp.sum(g2_recv[...].astype(F32), axis=0).astype(BF)
    z_bcast(f2_buf, F2)
    wait(g1_recv.at[pl.ds(0, G - 1)], recv.at[G1])
    f1_buf[s] = jnp.sum(g1_recv[...].astype(F32), axis=0).astype(BF)
    z_bcast(f1_buf, F1)

    pltpu.make_async_copy(lo_scr.at[par], lo_ref, here.at[O_LO]).wait()
    pltpu.make_async_copy(ud.at[par], ug_ref, here.at[O_UG]).wait()
    wait(a_buf.at[pl.ds(0, C - 1), 0], send.at[A])
    wait(a2_buf.at[pl.ds(0, C - 1), 0], send.at[A2])
    wait(a2_buf.at[:, 0], send.at[AS2])
    wait(b_buf.at[pl.ds(0, C - 1), 0], send.at[B])
    wait(a_buf.at[:, 0], send.at[AS])
    wait(b_buf.at[:, 0], send.at[BS])
    wait(pe_buf.at[:, 0], send.at[PES])
    for j in range(3):
        wait(pe_buf.at[pl.ds(0, per), 0], send.at[PE + j])
    for q in range(Q):
        wait(pair_recv.at[pl.ds(0, CQ)], send.at[PAIR + q])
    wait(rs_recv.at[pl.ds(0, C - 1)], send.at[RS])
    for buf, i in ((qr_buf, QKV), (at_recv, ATT), (zl_buf, ZL), (za_buf, ZA)):
        wait(buf.at[pl.ds(0, S - 1)], send.at[i])
    wait(h1_buf.at[pl.ds(0, S - 1)], send.at[H1])
    wait(h2_buf.at[0], send.at[H2])
    wait(sl2_buf.at[0], send.at[SL2])
    wait(h256.at[0], send.at[HX])
    wait(nx_buf.at[0], send.at[NX])
    wait(dn_recv, send.at[DN])
    wait(ud_recv, send.at[UD])
    wait(lg_buf.at[pl.ds(0, G - 1)], send.at[GL])
    wait(g1_recv.at[pl.ds(0, G - 1)], send.at[G1])
    wait(g2_recv.at[pl.ds(0, G - 1)], send.at[G2])
    wait(w2r_buf.at[:, 0], send.at[W2S])

    @pl.when(source)
    def _():
        wait(b_buf.at[pl.ds(0, C - 1)], send.at[W2])

    wait(f2_buf.at[pl.ds(0, S - 1)], recv.at[F2])
    for t in range(S):
        gf_ref[:, 128 * t : 128 * (t + 1)] = f2_buf[t].astype(F32)
    wait(f1_buf.at[pl.ds(0, S - 1)], recv.at[F1])
    for t in range(S):
        gm_ref[:, 128 * t : 128 * (t + 1)] = f1_buf[t, :rows].astype(F32)
        gl_ref[half * (t // 4) : half * (t // 4 + 1), 128 * (t % 4) : 128 * (t % 4 + 1)] = f1_buf[t, rows:].astype(F32)
    wait(f1_buf.at[pl.ds(0, S - 1)], send.at[F1])
    wait(f2_buf.at[pl.ds(0, S - 1)], send.at[F2])


def tail(*refs):
    ins, outs, mids = refs[:6], refs[6:12], refs[12:18]
    sem = refs[18]
    for i in range(6):
        pltpu.make_async_copy(ins[i], mids[i], sem.at[i]).start()
    for i in range(6):
        pltpu.make_async_copy(ins[i], mids[i], sem.at[i]).wait()
        if i == 1:
            outs[1][0, 0] = jnp.max(mids[1][...])
        else:
            pltpu.make_async_copy(mids[i], outs[i], sem.at[6 + i]).start()
    for i in (0, 2, 3, 4, 5):
        pltpu.make_async_copy(mids[i], outs[i], sem.at[6 + i]).wait()


def local(history, lengths, next_items, negatives, input_weight, output_weight, pool_features,
          tower_first, tower_middle, tower_last, S, G):
    events = history[0]
    tok = events.shape[0]
    C = G // 2
    R = pool_features.shape[0]
    RH = R // 2
    rows = tower_first.shape[0]
    V = pltpu.VMEM
    vmem = pl.BlockSpec(memory_space=pltpu.VMEM)
    hbm = pl.BlockSpec(memory_space=pltpu.HBM)
    width = G * RH // 4
    scratch = [
        pltpu.SemaphoreType.DMA((N_SEM,)),
        pltpu.SemaphoreType.DMA((N_SEM,)),
        pltpu.SemaphoreType.DMA((N_HERE,)),
        V((2, tok, 512), BF),
        V((2, 1, tok), jnp.int32),
        V((1, negatives.shape[1]), jnp.int32),
        V(input_weight.shape, BF),
        V(output_weight.shape, BF),
        V(pool_features.shape, BF),
        V((C, 2, rows, 128), BF),
        V((C, 2, 4, rows, 128), BF),
        V((C, 2, rows, 512), BF),
        V((2, 2, rows, 1024), BF),
        V((S, tok + tok // 2, 128), BF),
        V((S, tok + tok // 2, 128), BF),
        V((2 * tok, 512), BF),
        V((S * tok, DH), BF),
        V((S * tok, DH), BF),
        V((S * tok, DH), BF),
        V((S // 2, tok, 128), BF),
        V((S, tok, 128), BF),
        V((S, R, 128), BF),
        V((2, 4, R, 128), BF),
        V((2, 4, R, 128), BF),
        V((R, 128), F32),
        V((R, 512), F32),
        V((R, 128), F32),
        V((C, 2, RH, 512), BF),
        V((4, width, 2 * tok), F32),
        V((4, width, 2 * tok), BF),
        V((C, 2, RH, 512), BF),
        V((C, RH, 512), BF),
        V((C, RH, 512), BF),
        V((C, RH, 512), BF),
        V((8, 2 * tok), F32),
        V((8, 2 * tok), F32),
        V((2, tok, 512), F32),
        V((tok, 512), BF),
        V((tok, 512), BF),
        V((2, tok, 512), BF),
        V((S, 8, 128), F32),
        V((G, 8, 128), F32),
        V((S, RH, 512), BF),
        V((R, 512), BF),
        V((R, 1024), BF),
        V((G, 2, rows // 2, 128), BF),
        V((G, rows + rows // 2, 128), BF),
        V((G, rows + rows // 2, 128), BF),
        V((G, rows, 128), BF),
        V((G, rows, 128), BF),
        V((S, rows + rows // 2, 128), BF),
        V((S, rows, 128), BF),
        V((G * RH, 128), F32),
        V((2, tok, 512), F32),
        V((2, tok, 128), F32),
    ]
    shapes = [
        jax.ShapeDtypeStruct((tok, 512), BF),
        jax.ShapeDtypeStruct((8, 128), F32),
        jax.ShapeDtypeStruct((tok, 512), F32),
        jax.ShapeDtypeStruct((rows, 1024), F32),
        jax.ShapeDtypeStruct((rows, 1024), F32),
        jax.ShapeDtypeStruct((rows, 512), F32),
    ]
    results = pl.pallas_call(
        functools.partial(kernel, S, G),
        out_shape=shapes,
        in_specs=[pl.BlockSpec(memory_space=pltpu.SMEM)] + [hbm] * 9,
        out_specs=[hbm, vmem, hbm, vmem, vmem, vmem],
        scratch_shapes=scratch,
        compiler_params=pltpu.CompilerParams(
            collective_id=0, has_side_effects=True, vmem_limit_bytes=56 * 1024 * 1024),
    )(lengths, events, next_items, negatives, input_weight, output_weight, pool_features,
      tower_first, tower_middle, tower_last)
    lo, loss, ug, gf, gm, gl = pl.pallas_call(
        tail,
        out_shape=shapes[:1] + [jax.ShapeDtypeStruct((1, 1), F32)] + shapes[2:],
        in_specs=[hbm] * 6,
        out_specs=[hbm, pl.BlockSpec(memory_space=pltpu.SMEM)] + [hbm] * 4,
        scratch_shapes=[V(x.shape, x.dtype) for x in shapes] + [pltpu.SemaphoreType.DMA((12,))],
        compiler_params=pltpu.CompilerParams(vmem_limit_bytes=56 * 1024 * 1024),
    )(*results)
    return lo[None], loss.reshape(()), ug[None], gf, gm, gl


def solution(mesh):
    placed = (
        P("grp", "seq", None), P("grp"), P("grp", "seq"), P("grp", None), P(), P(),
        P("grp", None), P("grp", None), P("grp", None), P("grp", None),
    )
    return jax.shard_map(
        functools.partial(local, S=mesh.shape["seq"], G=mesh.shape["grp"]),
        mesh=mesh,
        in_specs=placed,
        out_specs=(
            P("grp", "seq", None), P(), P("grp", "seq", None),
            P("grp", None), P("grp", None), P("grp", None),
        ),
        check_vma=False,
    )
```

time: 110 us -> 85.1 us (0.77)
  Pallas kernels: 96.2 us -> 83.7 us
  local copies, waits for them, and re-layouts: 12 us -> 0 us
    pallas_call x1 -> x2, Pallas kernels: 96.2 us -> 83.7 us  [the longest x1 81.2 us: local(): pl.pallas_call(functools.partial(kernel, S, G), out_shape=shapes, in_spec...]
    unnamed x23 -> x0, local copies, waits for them, and re-layouts: 11.5 us -> none
where the time goes in v2:
time: 85.1 us; the launch traced here: 84.9 us
  Pallas kernels  83.7 us (98%)
  between operations  1.29 us (2%)
    pallas_call x1, Pallas kernels, local(): pl.pallas_call(functools.partial(kernel, S, G), out_shape=shapes, in_spec...  81.2 us
    pallas_call x1, Pallas kernels, local(): pl.pallas_call(tail, out_shape=shapes[:1] + [jax.ShapeDtypeStruct((1, 1),...  2.45 us

profile of v2, /device:TPU:1, one launch (start us, length us, event | category | flops | bytes accessed | tf_op | source)
XLA Modules:
  0.0 84.9 jit_solution(15176563816671866601)
XLA Ops:
  1.3 81.2 %shard_map.145 = (bf16[128,512]{1,0:T(8,128)(2,1)}, f32[8,128]{1,0:T(8,128)}, f32[128,512]{1,0:T(8,128)}, f32[32,1024]{1,0:T(8,128)}, f32[32,1024]{1,0:T(8,128)}, /*index=5*/f32[32,512]{1,0:T(8,128)}) custom-call(s32[1]{0:T(128)S(6)} %copy.16.len_ref, bf16[128,512]{1,0:T(8,128)(2,1)} %bitcast.4, s32[1,128]{1,0:T(1,128)} %nxt.1, s32[1,512]{1,0:T(1,128)} %neg.1, ...), custom_call_target="tpu_custom_call" | custom-call | tf_op jit(solution)/shard_map/pallas_call | solution.py:581
  82.5 2.4 %shard_map.146 = (bf16[128,512]{1,0:T(8,128)(2,1)}, f32[1,1]{1,0:T(1,128)}, f32[128,512]{1,0:T(8,128)}, f32[32,1024]{1,0:T(8,128)}, f32[32,1024]{1,0:T(8,128)}, /*index=5*/f32[32,512]{1,0:T(8,128)}) custom-call(bf16[128,512]{1,0:T(8,128)(2,1)} %get-tuple-element.18.refs_0_, f32[8,128]{1,0:T(8,128)} %get-tuple-element.19.refs_1_, ...), custom_call_target="tpu_custom_call" | custom-call | tf_op jit(solution)/shard_map/pallas_call | solution.py:591

commit v3 on v2

--- a/solution.py
+++ b/solution.py
@@ -16,9 +16,9 @@
 BF = jnp.bfloat16
 F32 = jnp.float32
 
-(A, A2, B, AS, AS2, BS, QKV, ATT, H1, H2, SL2, PES, HX, NX, DN, UD, ZA, ZL, GL, G1, G2, F1, F2, RS, W2, W2S) = range(26)
-PE, PAIR = 26, 29
-N_SEM = 34
+(A, A2, B, AS, AS2, BS, QKV, ATT, H1, H2, SL2, NX, NG, UP, US, UT, DN, UDS, UDP, ZA, ZL, GL, GP1, GP2, G1, G2, F1, F2,
+ RS, W2, W2S, PE) = range(32)
+N_SEM = 32
 
 (I_W3, I_H, I_WIN, I_WOUT, I_X, I_NEG, I_NXT, I_W2R, O_LO, O_UG) = range(10)
 I_W1, I_W2 = 10, 11
@@ -62,11 +62,11 @@
     len_ref, hist, nxt, neg, win, wout, xf, w1, w2, w3,
     lo_ref, loss_ref, ug_ref, gf_ref, gm_ref, gl_ref,
     send, recv, here,
-    h256, nx_buf, neg_v, win_v, wout_v, xf_v,
+    hist_v, nx_buf, neg_buf, win_v, wout_v, xf_v,
     a_buf, a2_buf, b_buf, w2r_buf, qs_buf, qr_buf, gate, k_scr, q_scr, v_scr, at_send, at_recv,
-    h1_buf, h2_buf, sl2_buf, pre1, ui, inv, pe_buf, em, st, pt_send, pair_recv, rs_send, rs_recv,
-    dn_send, dn_recv, ud, ud_send, ud_recv, lo_scr, zl_buf, lg_buf, za_buf, rg, sg_scr,
-    gl_scr, g1_send, g1_recv, g2_send, g2_recv, f1_buf, f2_buf, cnt, uu, uinv,
+    h1_buf, h2_buf, sl2_buf, pre1, ui, inv, pe_buf, em, st, rs_send, rs_recv, u_buf,
+    dn_buf, ud, uds_send, uds_recv, udp_send, udp_recv, lo_scr, zl_buf, lg_buf, za_buf, rg, sg_scr,
+    gl_scr, gp1, gp1_recv, gp2, gp2_recv, g1_send, g1_recv, g2_send, g2_recv, f1_buf, f2_buf, cnt, uu, uinv,
 ):
     C = G // 2
     s = lax.axis_index("seq")
@@ -74,15 +74,18 @@
     p = g // 2
     c = g % 2
     par = s % 2
-    tok = h256.shape[1]
+    tok = hist_v.shape[0]
+    me = 2 * c + par
     rows = b_buf.shape[2]
     NB = a2_buf.shape[2]
     half = rows // 2
+    NEG = neg.shape[1]
     R = xf_v.shape[0]
     RH = R // 2
     length = len_ref[0]
     pair = (s + 1 - 2 * par, g)
     sib = (s, 2 * p + 1 - c)
+    diag = (s + 1 - 2 * par, 2 * p + 1 - c)
     cols = pl.ds(pl.multiple_of(s * 128, 128), 128)
 
     def copy(src, dst, i, dev):
@@ -105,12 +108,17 @@
             return 0
         lax.fori_loop(1, C, step, 0)
 
-    def grp_scatter(src, dst, i):
+    def chip_scatter(src, dst, i):
         def step(k, _):
-            t = lax.rem(g + k, G)
-            copy(src.at[t], dst.at[g], i, (s, t)).start()
+            t = lax.rem(p + k, C)
+            copy(src.at[t], dst.at[p], i, (s, 2 * t + c)).start()
             return 0
-        lax.fori_loop(1, G, step, 0)
+        lax.fori_loop(1, C, step, 0)
+        dst[p] = src[p]
+
+    def quad(buf, i):
+        for dev in (sib, pair, diag):
+            copy(buf.at[me], buf.at[me], i, dev).start()
 
     barrier = pltpu.get_barrier_semaphore()
 
@@ -124,17 +132,18 @@
 
     lax.fori_loop(1, G, greet_grp, 0)
     lax.fori_loop(1, S, greet_seq, 0)
-
-    fetch(hist, h256.at[par], I_H)
+    pl.semaphore_signal(barrier, inc=1, device_id=diag, device_id_type=MESH)
+
     fetch(w1.at[:, cols], a_buf.at[p, c], I_W1)
     for j in range(NB):
         block = pl.ds(pl.multiple_of((2 * j + par) * 128, 128), 128)
         fetch(w2.at[:, block], a2_buf.at[p, c, j], I_W2 + j)
+    fetch(hist, hist_v, I_H)
     fetch(win, win_v, I_WIN)
-    fetch(nxt, nx_buf.at[par], I_NXT)
+    fetch(nxt, nx_buf.at[me], I_NXT)
     fetch(w3, b_buf.at[p, c], I_W3)
     fetch(xf, xf_v, I_X)
-    fetch(neg, neg_v, I_NEG)
+    fetch(neg, neg_buf.at[c, :, pl.ds(0, NEG)], I_NEG)
     fetch(wout, wout_v, I_WOUT)
     source = p // 2 == s
 
@@ -142,8 +151,13 @@
     def _():
         fetch(w2, w2r_buf.at[p % 2, c], I_W2R)
 
-    wait(h256.at[par], here.at[I_H])
-    normed = layer_norm(h256[par].astype(F32)).astype(BF)
+    neg_buf[c, :, NEG:] = jnp.full((1, 128), length, jnp.int32)
+    wait(a_buf.at[p, c], here.at[I_W1])
+    pl.semaphore_wait(barrier, (G - 1) + (S - 1) + 1)
+    chips(a_buf.at[p, c], a_buf.at[p, c], A)
+
+    wait(hist_v, here.at[I_H])
+    normed = layer_norm(hist_v[...].astype(F32)).astype(BF)
     wait(win_v, here.at[I_WIN])
     for j in range(4):
         x = silu(dot(normed, win_v[:, 512 + 384 * j : 512 + 384 * (j + 1)])).astype(BF)
@@ -152,14 +166,6 @@
             qs_buf[2 * j + e, :tok] = x[:, o : o + 128]
             v = x[:, o + 128 : o + 192]
             qs_buf[2 * j + e, tok:] = jnp.concatenate([v[: tok // 2], v[tok // 2 :]], axis=1)
-    wait(a_buf.at[p, c], here.at[I_W1])
-    for j in range(NB):
-        wait(a2_buf.at[p, c, j], here.at[I_W2 + j])
-    wait(nx_buf.at[par], here.at[I_NXT])
-    wait(b_buf.at[p, c], here.at[I_W3])
-    pl.semaphore_wait(barrier, (G - 1) + (S - 1))
-
-    chips(a_buf.at[p, c], a_buf.at[p, c], A)
 
     def qkv_step(k, _):
         t = lax.rem(s + k, S)
@@ -168,35 +174,41 @@
 
     lax.fori_loop(1, S, qkv_step, 0)
     qr_buf[s] = qs_buf[s]
-
-    def local_row(ids):
-        mine = (ids // RH) % 2 == par
-        return jnp.where(mine, (ids // R) * RH + ids % RH, -1)
-
-    wait(neg_v, here.at[I_NEG])
-    n_rows = G * RH
-    ids = local_row(neg_v[...])
-    hot = (lax.broadcasted_iota(jnp.int32, (n_rows, ids.shape[1]), 0) == ids).astype(F32).astype(BF)
-    cnt[...] = dot(hot, jnp.ones((ids.shape[1], 128), BF))
-
+    for j in range(NB):
+        wait(a2_buf.at[p, c, j], here.at[I_W2 + j])
     chips(a2_buf.at[p, c], a2_buf.at[p, c], A2)
+    wait(nx_buf.at[me], here.at[I_NXT])
+    quad(nx_buf, NX)
+    wait(neg_buf.at[c, :, pl.ds(0, NEG)], here.at[I_NEG])
+    copy(neg_buf.at[c], neg_buf.at[c], NG, sib).start()
+    gate[...] = silu(dot(normed, win_v[:, :512])).astype(BF)
+
     wait(xf_v, here.at[I_X])
     wait(a_buf.at[pl.ds(0, C - 1), 0], recv.at[A])
     copy(a_buf.at[:, c], a_buf.at[:, c], AS, sib).start()
+    wait(b_buf.at[p, c], here.at[I_W3])
+    chips(b_buf.at[p, c], b_buf.at[p, c], B)
     wait(a_buf.at[:, 0], recv.at[AS])
     z1 = dot(xf_v[...], a_buf[...].reshape(G * rows, 128))
     pre1[...] = z1
     h1_buf[s] = silu(z1).astype(BF)
     z_bcast(h1_buf, H1)
+
+    def local_row(ids):
+        return jnp.where((ids // RH) % 4 == me, (ids // (2 * R)) * RH + ids % RH, -1)
+
+    wait(neg_buf.at[0], recv.at[NG])
+    n_rows = C * RH
+    for e in (0, 1):
+        ids = local_row(neg_buf[e, :, :NEG])
+        hot = (lax.broadcasted_iota(jnp.int32, (n_rows, NEG), 0) == ids).astype(F32).astype(BF)
+        cnt[e] = dot(hot, jnp.ones((NEG, 128), BF))
     def whole(buf):
         return jnp.concatenate([buf[j % 2, j // 2] for j in range(2 * NB)], axis=1)
 
     wait(a2_buf.at[pl.ds(0, C - 1), 0], recv.at[A2])
     copy(a2_buf.at[:, c], a2_buf.at[:, c], AS2, sib).start()
-    chips(b_buf.at[p, c], b_buf.at[p, c], B)
     wait(qr_buf.at[pl.ds(0, S - 1)], recv.at[QKV])
-    copy(h256.at[par], h256.at[par], HX, pair).start()
-    copy(nx_buf.at[par], nx_buf.at[par], NX, pair).start()
     for j in range(S):
         x = qr_buf[j]
         q_scr[tok * j : tok * (j + 1)] = x[:tok, :DH]
@@ -219,11 +231,13 @@
             acc = acc + dot(w.astype(BF), v_scr[W * kb : W * (kb + 1)])
         pos = W * b + lax.broadcasted_iota(jnp.int32, (W, 1), 0)
         acc = jnp.where(pos < length, acc, 0.0).astype(BF)
-        at_send[b] = jnp.concatenate([acc[:tok], acc[tok:]], axis=1)
+        for i in (0, 1):
+            o = acc[tok * i : tok * (i + 1)]
+            at_send[2 * b + i] = jnp.concatenate([o[: tok // 2], o[tok // 2 :]], axis=1)
 
     for b in reversed(range(S // 2)):
         attend(b)
-    at_recv[s] = at_send[s // 2]
+    at_recv[s] = at_send[s]
 
     wait(h1_buf.at[pl.ds(0, S - 1)], recv.at[H1])
     wait(a2_buf.at[:, 0], recv.at[AS2])
@@ -236,14 +250,11 @@
 
     def at_step(k, _):
         t = lax.rem(s + k, S)
-        copy(at_send.at[t // 2], at_recv.at[s], ATT, (t, g)).start()
+        copy(at_send.at[t], at_recv.at[s], ATT, (t, g)).start()
         return 0
 
     lax.fori_loop(1, S, at_step, 0)
-    wait(h256.at[0], recv.at[HX])
     copy(sl2_buf.at[par], sl2_buf.at[par], SL2, pair).start()
-    both = h256[...].reshape(2 * tok, 512)
-    gate[...] = silu(dot(layer_norm(both.astype(F32)).astype(BF), win_v[:, :512])).astype(BF)
 
     wait(b_buf.at[pl.ds(0, C - 1), 0], recv.at[B])
     copy(b_buf.at[:, c], b_buf.at[:, c], BS, sib).start()
@@ -256,17 +267,8 @@
     unit_item = raw * item_inverse
     ui[...] = unit_item
     inv[...] = jnp.broadcast_to(item_inverse, inv.shape)
-    pe_buf[p, c] = ui[pl.ds(pl.multiple_of(par * RH, RH), RH)].astype(BF)
-
-    copy(pe_buf.at[p, c], pe_buf.at[p, c], PES, sib).start()
-    per = (C - 1) // 3
-
-    def pe_step(k, _):
-        t = lax.rem(p + k, C)
-        copy(pe_buf.at[p, c], pe_buf.at[p, c], PE + (k - 1) // per, (s, 2 * t + c)).start()
-        return 0
-
-    lax.fori_loop(1, C, pe_step, 0)
+    pe_buf[p] = ui[pl.ds(pl.multiple_of(par * RH, RH), RH)].astype(BF)
+    chips(pe_buf.at[p], pe_buf.at[p], PE)
 
     @pl.when(source)
     def _():
@@ -283,54 +285,55 @@
     merged = jnp.concatenate(
         [jnp.concatenate(tops, axis=1), jnp.concatenate(bottoms, axis=1)], axis=0).astype(F32)
     branch = (layer_norm(merged) * gate[...].astype(F32)).astype(BF)
-    layer_out = (h256[...].reshape(2 * tok, 512).astype(F32) + dot(branch, wout_v[...])).astype(BF)
-    lo_scr[...] = layer_out.reshape(2, tok, 512)
-    pltpu.make_async_copy(lo_scr.at[par], lo_ref, here.at[O_LO]).start()
+    layer_out = (hist_v[...].astype(F32) + dot(branch, wout_v[...])).astype(BF)
+    lo_scr[...] = layer_out
+    pltpu.make_async_copy(lo_scr, lo_ref, here.at[O_LO]).start()
     outward = layer_out.astype(F32)
     user_inverse = lax.rsqrt(jnp.sum(outward * outward, axis=-1, keepdims=True) + EPS_UNIT)
     unit_user = outward * user_inverse
-    unit_low = unit_user.astype(BF)
-    uu[...] = unit_user.reshape(2, tok, 512)
-    uinv[...] = jnp.broadcast_to(user_inverse, (2 * tok, 128)).reshape(2, tok, 128)
-
-    wait(nx_buf.at[0], recv.at[NX])
-    items = local_row(jnp.concatenate([nx_buf[0], nx_buf[1]], axis=1))
-    pair_pos = lax.broadcasted_iota(jnp.int32, (1, W), 1)
-    positions = (s // 2) * W + pair_pos
-    valid = (positions < length - 1).astype(F32)
-
-    for j in range(3):
-        wait(pe_buf.at[pl.ds(0, per), 0], recv.at[PE + j])
-
-        def fwd(k, _):
-            t = lax.rem(p + C - k, C)
-            copy(pe_buf.at[t, c], pe_buf.at[t, c], PES, sib).start()
-            return 0
-
-        lax.fori_loop(1 + per * j, 1 + per * (j + 1), fwd, 0)
-
-    wait(pe_buf.at[:, 0], recv.at[PES])
+    u_buf[me] = unit_user.astype(BF)
+    copy(u_buf.at[me], u_buf.at[me], UP, pair).start()
+    copy(u_buf.at[me], u_buf.at[me], US, sib).start()
+    uu[...] = unit_user
+    uinv[...] = jnp.broadcast_to(user_inverse, (tok, 128))
+
+    P4 = 4 * tok
+    wait(nx_buf.at[pl.ds(0, 3)], recv.at[NX])
+    items = local_row(jnp.concatenate([nx_buf[j] for j in range(4)], axis=1))
+    quad_pos = lax.broadcasted_iota(jnp.int32, (1, P4), 1)
+    positions = (s // 2) * W + quad_pos % W
+    lens = jnp.concatenate([neg_buf[j // 2, :, NEG:] for j in range(4)], axis=1)
+    valid = (positions < lens - 1).astype(F32)
+
+    wait(u_buf.at[0], recv.at[UP])
+    other = 2 * c + 1 - par
+    copy(u_buf.at[other], u_buf.at[other], UT, sib).start()
+    wait(pe_buf.at[pl.ds(0, C - 1)], recv.at[PE])
+    wait(u_buf.at[0], recv.at[US])
+    wait(u_buf.at[0], recv.at[UT])
 
     Q = 4
     CQ = C // Q
     width = n_rows // Q
-    row_id = lax.broadcasted_iota(jnp.int32, (width, W), 0)
-    den = jnp.zeros((1, W), F32)
-    positive = jnp.zeros((1, W), F32)
+    users = u_buf[...].reshape(P4, 512)
+    row_id = lax.broadcasted_iota(jnp.int32, (width, P4), 0)
+    den = jnp.zeros((1, P4), F32)
+    positive = jnp.zeros((1, P4), F32)
     for q in range(Q):
-        logit = TEMP * dot_t(pe_buf[CQ * q : CQ * (q + 1)].reshape(width, 512), unit_low)
+        logit = TEMP * dot_t(pe_buf[CQ * q : CQ * (q + 1)].reshape(width, 512), users)
         own = row_id + width * q == items
-        times = cnt[width * q : width * (q + 1)]
-        e = jnp.where(own, 0.0, jnp.exp(logit) * jnp.concatenate([times] * (W // 128), axis=1))
+        times = jnp.concatenate([cnt[j // 2, width * q : width * (q + 1)] for j in range(4)], axis=1)
+        e = jnp.where(own, 0.0, jnp.exp(logit) * times)
         em[q] = e
         den = den + jnp.sum(e, axis=0, keepdims=True)
         positive = positive + jnp.sum(jnp.where(own, logit, 0.0), axis=0, keepdims=True)
-    row8 = lax.broadcasted_iota(jnp.int32, (8, W), 0)
-    dn_send[...] = jnp.where(row8 == 0, den, positive)
-    copy(dn_send, dn_recv, DN, pair).start()
-    wait(dn_recv, recv.at[DN])
-    den = den + dn_recv[0:1]
-    positive = positive + dn_recv[1:2]
+    row8 = lax.broadcasted_iota(jnp.int32, (8, P4), 0)
+    dn_buf[me] = jnp.where(row8 == 0, den, positive)
+    quad(dn_buf, DN)
+    wait(dn_buf.at[pl.ds(0, 3)], recv.at[DN])
+    sums = dn_buf[0] + dn_buf[1] + dn_buf[2] + dn_buf[3]
+    den = sums[0:1]
+    positive = sums[1:2]
     positive_exp = jnp.exp(positive)
     den = den + positive_exp
     slope = valid * (positive_exp / den - 1.0)
@@ -340,14 +343,7 @@
         gq = lax.rem(p // CQ + q, Q)
         sm = jnp.where(row_id + width * gq == items, slope, scale * em[gq]).astype(BF)
         st[gq] = sm
-        pt_send[pl.ds(CQ * gq, CQ)] = (TEMP * dot(sm, unit_low)).astype(BF).reshape(CQ, 2, RH, 512)
-        copy(pt_send.at[pl.ds(CQ * gq, CQ), 1 - c], pair_recv.at[pl.ds(CQ * gq, CQ)], PAIR + q, sib).start()
-
-    for q in range(Q):
-        gq = lax.rem(p // CQ + q, Q)
-        wait(pair_recv.at[pl.ds(CQ * gq, CQ)], recv.at[PAIR + q])
-        chip_sum = pt_send[pl.ds(CQ * gq, CQ), c].astype(F32) + pair_recv[pl.ds(CQ * gq, CQ)].astype(F32)
-        rs_send[pl.ds(CQ * gq, CQ)] = chip_sum.astype(BF)
+        rs_send[pl.ds(CQ * gq, CQ)] = (TEMP * dot(sm, users)).astype(BF).reshape(CQ, RH, 512)
 
         def rs_step(i, _):
             t = CQ * gq + lax.rem(p + i, CQ)
@@ -359,17 +355,17 @@
 
         lax.fori_loop(0, CQ, rs_step, 0)
 
-    mine = pair_pos // tok == par
+    mine = quad_pos // tok == me
     loss_sum = jnp.sum(jnp.where(mine, valid * (jnp.log(den) - positive), 0.0))
     lane = lax.broadcasted_iota(jnp.int32, (8, 128), 1)
     count = jnp.full((8, 128), length - 1, jnp.int32).astype(F32)
     zl_buf[s] = jnp.where(lane == 0, loss_sum, jnp.where(lane == 1, count, 0.0))
     z_bcast(zl_buf, ZL)
 
-    user_dir = t_dot(st[...].reshape(n_rows, W), pe_buf[...].reshape(n_rows, 512))
-    ud[...] = user_dir.reshape(2, tok, 512)
-    ud_send[...] = ud[1 - par].astype(BF)
-    copy(ud_send, ud_recv, UD, pair).start()
+    user_dir = t_dot(st[...].reshape(n_rows, P4), pe_buf[...].reshape(n_rows, 512))
+    ud[...] = user_dir.reshape(2, 2, tok, 512)
+    uds_send[...] = ud[1 - c].astype(BF)
+    copy(uds_send, uds_recv, UDS, sib).start()
 
     @pl.when(source)
     def _():
@@ -380,6 +376,9 @@
         wait(w2r_buf.at[:, 0], recv.at[W2])
 
     copy(w2r_buf.at[:, c], w2r_buf.at[:, c], W2S, sib).start()
+    wait(uds_recv, recv.at[UDS])
+    udp_send[...] = (ud[c, 1 - par] + uds_recv[1 - par].astype(F32)).astype(BF)
+    copy(udp_send, udp_recv, UDP, pair).start()
 
     wait(rs_recv.at[pl.ds(0, C - 1)], recv.at[RS])
     rs_recv[p] = rs_send[p]
@@ -394,11 +393,11 @@
         return 0
 
     lax.fori_loop(1, G, lg_step, 0)
-    wait(ud_recv, recv.at[UD])
-    user_dir = TEMP * (ud[par] + ud_recv[...].astype(F32))
-    uun = uu[par]
-    ud[par] = uinv[par][:, :1] * (user_dir - uun * jnp.sum(uun * user_dir, axis=-1, keepdims=True))
-    pltpu.make_async_copy(ud.at[par], ug_ref, here.at[O_UG]).start()
+    wait(udp_recv, recv.at[UDP])
+    user_dir = TEMP * (ud[c, par] + uds_recv[par].astype(F32) + udp_recv[...].astype(F32))
+    uun = uu[...]
+    uu[...] = uinv[:, :1] * (user_dir - uun * jnp.sum(uun * user_dir, axis=-1, keepdims=True))
+    pltpu.make_async_copy(uu, ug_ref, here.at[O_UG]).start()
     wait(w2r_buf.at[:, 0], recv.at[W2S])
     wait(sl2_buf.at[0], recv.at[SL2])
     h1 = jnp.concatenate([h1_buf[j] for j in range(S)], axis=1)
@@ -420,15 +419,19 @@
     sg = (dot_t(raw_grad, b_buf[...].reshape(G * rows, 512)) * slope2).astype(BF)
     sg_scr[...] = sg
     fg = (dot_t(sg, w2r_buf[...].reshape(4 * rows, 1024)) * slope1).astype(BF)
-    g2_send[...] = t_dot(xf_v[...], fg).astype(BF).reshape(G, rows, 128)
-    grp_scatter(g2_send, g2_recv, G2)
-    g2_recv[g] = g2_send[g]
+    gp2[...] = t_dot(xf_v[...], fg).astype(BF).reshape(C, 2, rows, 128)
+    copy(gp2.at[:, 1 - c], gp2_recv, GP2, sib).start()
     q_cols = pl.ds(pl.multiple_of(lax.rem(s, 4) * 128, 128), 128)
-    gl_scr[...] = t_dot(h2, rg[:, q_cols]).astype(BF).reshape(G, 2, half, 128)
-    g1_send[:, :rows] = t_dot(h1, sg_scr[:, cols]).astype(BF).reshape(G, rows, 128)
-    g1_send[:, rows:] = gl_scr[:, s // 4]
-    grp_scatter(g1_send, g1_recv, G1)
-    g1_recv[g] = g1_send[g]
+    gl_scr[...] = t_dot(h2, rg[:, q_cols]).astype(BF).reshape(C, 2, 2, half, 128)
+    gp1[:, :, :rows] = t_dot(h1, sg_scr[:, cols]).astype(BF).reshape(C, 2, rows, 128)
+    gp1[:, :, rows:] = gl_scr[:, :, s // 4]
+    copy(gp1.at[:, 1 - c], gp1_recv, GP1, sib).start()
+    wait(gp2_recv, recv.at[GP2])
+    g2_send[...] = (gp2[:, c].astype(F32) + gp2_recv[...].astype(F32)).astype(BF)
+    chip_scatter(g2_send, g2_recv, G2)
+    wait(gp1_recv, recv.at[GP1])
+    g1_send[...] = (gp1[:, c].astype(F32) + gp1_recv[...].astype(F32)).astype(BF)
+    chip_scatter(g1_send, g1_recv, G1)
 
     wait(lg_buf.at[pl.ds(0, G - 1)], recv.at[GL])
     total = jnp.sum(lg_buf[...], axis=0)
@@ -436,39 +439,40 @@
     denom = jnp.sum(jnp.where(lane == 1, total, 0.0), axis=1, keepdims=True)
     loss_ref[...] = jnp.broadcast_to(numer * S / denom, loss_ref.shape)
 
-    wait(g2_recv.at[pl.ds(0, G - 1)], recv.at[G2])
+    wait(g2_recv.at[pl.ds(0, C - 1)], recv.at[G2])
     f2_buf[s] = jnp.sum(g2_recv[...].astype(F32), axis=0).astype(BF)
     z_bcast(f2_buf, F2)
-    wait(g1_recv.at[pl.ds(0, G - 1)], recv.at[G1])
+    wait(g1_recv.at[pl.ds(0, C - 1)], recv.at[G1])
     f1_buf[s] = jnp.sum(g1_recv[...].astype(F32), axis=0).astype(BF)
     z_bcast(f1_buf, F1)
 
-    pltpu.make_async_copy(lo_scr.at[par], lo_ref, here.at[O_LO]).wait()
-    pltpu.make_async_copy(ud.at[par], ug_ref, here.at[O_UG]).wait()
+    pltpu.make_async_copy(lo_scr, lo_ref, here.at[O_LO]).wait()
+    pltpu.make_async_copy(uu, ug_ref, here.at[O_UG]).wait()
     wait(a_buf.at[pl.ds(0, C - 1), 0], send.at[A])
     wait(a2_buf.at[pl.ds(0, C - 1), 0], send.at[A2])
     wait(a2_buf.at[:, 0], send.at[AS2])
     wait(b_buf.at[pl.ds(0, C - 1), 0], send.at[B])
     wait(a_buf.at[:, 0], send.at[AS])
     wait(b_buf.at[:, 0], send.at[BS])
-    wait(pe_buf.at[:, 0], send.at[PES])
-    for j in range(3):
-        wait(pe_buf.at[pl.ds(0, per), 0], send.at[PE + j])
-    for q in range(Q):
-        wait(pair_recv.at[pl.ds(0, CQ)], send.at[PAIR + q])
+    wait(pe_buf.at[pl.ds(0, C - 1)], send.at[PE])
     wait(rs_recv.at[pl.ds(0, C - 1)], send.at[RS])
     for buf, i in ((qr_buf, QKV), (at_recv, ATT), (zl_buf, ZL), (za_buf, ZA)):
         wait(buf.at[pl.ds(0, S - 1)], send.at[i])
     wait(h1_buf.at[pl.ds(0, S - 1)], send.at[H1])
     wait(h2_buf.at[0], send.at[H2])
     wait(sl2_buf.at[0], send.at[SL2])
-    wait(h256.at[0], send.at[HX])
-    wait(nx_buf.at[0], send.at[NX])
-    wait(dn_recv, send.at[DN])
-    wait(ud_recv, send.at[UD])
+    wait(nx_buf.at[pl.ds(0, 3)], send.at[NX])
+    wait(neg_buf.at[0], send.at[NG])
+    for i in (UP, US, UT):
+        wait(u_buf.at[0], send.at[i])
+    wait(dn_buf.at[pl.ds(0, 3)], send.at[DN])
+    wait(uds_recv, send.at[UDS])
+    wait(udp_recv, send.at[UDP])
+    wait(gp1_recv, send.at[GP1])
+    wait(gp2_recv, send.at[GP2])
     wait(lg_buf.at[pl.ds(0, G - 1)], send.at[GL])
-    wait(g1_recv.at[pl.ds(0, G - 1)], send.at[G1])
-    wait(g2_recv.at[pl.ds(0, G - 1)], send.at[G2])
+    wait(g1_recv.at[pl.ds(0, C - 1)], send.at[G1])
+    wait(g2_recv.at[pl.ds(0, C - 1)], send.at[G2])
     wait(w2r_buf.at[:, 0], send.at[W2S])
 
     @pl.when(source)
@@ -512,14 +516,14 @@
     V = pltpu.VMEM
     vmem = pl.BlockSpec(memory_space=pltpu.VMEM)
     hbm = pl.BlockSpec(memory_space=pltpu.HBM)
-    width = G * RH // 4
+    width = C * RH // 4
     scratch = [
         pltpu.SemaphoreType.DMA((N_SEM,)),
         pltpu.SemaphoreType.DMA((N_SEM,)),
         pltpu.SemaphoreType.DMA((N_HERE,)),
-        V((2, tok, 512), BF),
-        V((2, 1, tok), jnp.int32),
-        V((1, negatives.shape[1]), jnp.int32),
+        V((tok, 512), BF),
+        V((4, 1, tok), jnp.int32),
+        V((2, 1, negatives.shape[1] + 128), jnp.int32),
         V(input_weight.shape, BF),
         V(output_weight.shape, BF),
         V(pool_features.shape, BF),
@@ -529,46 +533,50 @@
         V((2, 2, rows, 1024), BF),
         V((S, tok + tok // 2, 128), BF),
         V((S, tok + tok // 2, 128), BF),
-        V((2 * tok, 512), BF),
+        V((tok, 512), BF),
         V((S * tok, DH), BF),
         V((S * tok, DH), BF),
         V((S * tok, DH), BF),
-        V((S // 2, tok, 128), BF),
-        V((S, tok, 128), BF),
+        V((S, tok // 2, 128), BF),
+        V((S, tok // 2, 128), BF),
         V((S, R, 128), BF),
         V((2, 4, R, 128), BF),
         V((2, 4, R, 128), BF),
         V((R, 128), F32),
         V((R, 512), F32),
         V((R, 128), F32),
-        V((C, 2, RH, 512), BF),
-        V((4, width, 2 * tok), F32),
-        V((4, width, 2 * tok), BF),
-        V((C, 2, RH, 512), BF),
+        V((C, RH, 512), BF),
+        V((4, width, 4 * tok), F32),
+        V((4, width, 4 * tok), BF),
         V((C, RH, 512), BF),
         V((C, RH, 512), BF),
-        V((C, RH, 512), BF),
-        V((8, 2 * tok), F32),
-        V((8, 2 * tok), F32),
-        V((2, tok, 512), F32),
+        V((4, tok, 512), BF),
+        V((4, 8, 4 * tok), F32),
+        V((2, 2, tok, 512), F32),
+        V((2, tok, 512), BF),
+        V((2, tok, 512), BF),
         V((tok, 512), BF),
         V((tok, 512), BF),
-        V((2, tok, 512), BF),
+        V((tok, 512), BF),
         V((S, 8, 128), F32),
         V((G, 8, 128), F32),
         V((S, RH, 512), BF),
         V((R, 512), BF),
         V((R, 1024), BF),
-        V((G, 2, rows // 2, 128), BF),
-        V((G, rows + rows // 2, 128), BF),
-        V((G, rows + rows // 2, 128), BF),
-        V((G, rows, 128), BF),
-        V((G, rows, 128), BF),
+        V((C, 2, 2, rows // 2, 128), BF),
+        V((C, 2, rows + rows // 2, 128), BF),
+        V((C, rows + rows // 2, 128), BF),
+        V((C, 2, rows, 128), BF),
+        V((C, rows, 128), BF),
+        V((C, rows + rows // 2, 128), BF),
+        V((C, rows + rows // 2, 128), BF),
+        V((C, rows, 128), BF),
+        V((C, rows, 128), BF),
         V((S, rows + rows // 2, 128), BF),
         V((S, rows, 128), BF),
-        V((G * RH, 128), F32),
-        V((2, tok, 512), F32),
-        V((2, tok, 128), F32),
+        V((2, C * RH, 128), F32),
+        V((tok, 512), F32),
+        V((tok, 128), F32),
     ]
     shapes = [
         jax.ShapeDtypeStruct((tok, 512), BF),

time: 85.1 us -> 83.5 us (0.981)
  Pallas kernels: 83.7 us -> 82 us
    pallas_call x1, Pallas kernels: 81.2 us -> 79.6 us  [local(): pl.pallas_call(functools.partial(kernel, S, G), out_shape=shapes, in_spec...]
where the time goes in v3:
time: 83.5 us; the launch traced here: 83.3 us
  Pallas kernels  82 us (98%)
  between operations  1.29 us (2%)
    pallas_call x1, Pallas kernels, local(): pl.pallas_call(functools.partial(kernel, S, G), out_shape=shapes, in_spec...  79.6 us
    pallas_call x1, Pallas kernels, local(): pl.pallas_call(tail, out_shape=shapes[:1] + [jax.ShapeDtypeStruct((1, 1),...  2.45 us

profile of v3, /device:TPU:1, one launch (start us, length us, event | category | flops | bytes accessed | tf_op | source)
XLA Modules:
  0.0 83.3 jit_solution(6722530653382191351)
XLA Ops:
  1.3 79.6 %shard_map.145 = (bf16[128,512]{1,0:T(8,128)(2,1)}, f32[8,128]{1,0:T(8,128)}, f32[128,512]{1,0:T(8,128)}, f32[32,1024]{1,0:T(8,128)}, f32[32,1024]{1,0:T(8,128)}, /*index=5*/f32[32,512]{1,0:T(8,128)}) custom-call(s32[1]{0:T(128)S(6)} %copy.16.len_ref, bf16[128,512]{1,0:T(8,128)(2,1)} %bitcast.4, s32[1,128]{1,0:T(1,128)} %nxt.1, s32[1,512]{1,0:T(1,128)} %neg.1, ...), custom_call_target="tpu_custom_call" | custom-call | tf_op jit(solution)/shard_map/pallas_call | solution.py:589
  80.9 2.4 %shard_map.146 = (bf16[128,512]{1,0:T(8,128)(2,1)}, f32[1,1]{1,0:T(1,128)}, f32[128,512]{1,0:T(8,128)}, f32[32,1024]{1,0:T(8,128)}, f32[32,1024]{1,0:T(8,128)}, /*index=5*/f32[32,512]{1,0:T(8,128)}) custom-call(bf16[128,512]{1,0:T(8,128)(2,1)} %get-tuple-element.18.refs_0_, f32[8,128]{1,0:T(8,128)} %get-tuple-element.19.refs_1_, ...), custom_call_target="tpu_custom_call" | custom-call | tf_op jit(solution)/shard_map/pallas_call | solution.py:599

commit v4 on v3

--- a/solution.py
+++ b/solution.py
@@ -16,13 +16,14 @@
 BF = jnp.bfloat16
 F32 = jnp.float32
 
-(A, A2, B, AS, AS2, BS, QKV, ATT, H1, H2, SL2, NX, NG, UP, US, UT, DN, UDS, UDP, ZA, ZL, GL, GP1, GP2, G1, G2, F1, F2,
- RS, W2, W2S, PE) = range(32)
-N_SEM = 32
-
-(I_W3, I_H, I_WIN, I_WOUT, I_X, I_NEG, I_NXT, I_W2R, O_LO, O_UG) = range(10)
-I_W1, I_W2 = 10, 11
-N_HERE = 15
+(A, A2, B, AS, AS2, BS, QKV, ATT, H1, H2, SL2, NX, NG, UP, US, UT, DN, UDS, UDP, ZL, GL, GP1, GP2, G1, G2, F1, F2,
+ W2, PE) = range(29)
+RS, ZA = 29, 31
+N_SEM = 33
+
+(I_W3, I_H, I_WIN, I_WOUT, I_X, I_NEG, I_NXT, I_W1) = range(8)
+I_W2 = 8
+N_HERE = 12
 
 
 def silu(x):
@@ -65,7 +66,7 @@
     hist_v, nx_buf, neg_buf, win_v, wout_v, xf_v,
     a_buf, a2_buf, b_buf, w2r_buf, qs_buf, qr_buf, gate, k_scr, q_scr, v_scr, at_send, at_recv,
     h1_buf, h2_buf, sl2_buf, pre1, ui, inv, pe_buf, em, st, rs_send, rs_recv, u_buf,
-    dn_buf, ud, uds_send, uds_recv, udp_send, udp_recv, lo_scr, zl_buf, lg_buf, za_buf, rg, sg_scr,
+    dn_buf, ud, uds_send, uds_recv, udp_send, udp_recv, zl_buf, lg_buf, za_buf, rg, sg_scr,
     gl_scr, gp1, gp1_recv, gp2, gp2_recv, g1_send, g1_recv, g2_send, g2_recv, f1_buf, f2_buf, cnt, uu, uinv,
 ):
     C = G // 2
@@ -120,6 +121,7 @@
         for dev in (sib, pair, diag):
             copy(buf.at[me], buf.at[me], i, dev).start()
 
+    fetch(w1.at[:, cols], a_buf.at[p, c], I_W1)
     barrier = pltpu.get_barrier_semaphore()
 
     def greet_grp(k, _):
@@ -134,7 +136,6 @@
     lax.fori_loop(1, S, greet_seq, 0)
     pl.semaphore_signal(barrier, inc=1, device_id=diag, device_id_type=MESH)
 
-    fetch(w1.at[:, cols], a_buf.at[p, c], I_W1)
     for j in range(NB):
         block = pl.ds(pl.multiple_of((2 * j + par) * 128, 128), 128)
         fetch(w2.at[:, block], a2_buf.at[p, c, j], I_W2 + j)
@@ -145,12 +146,6 @@
     fetch(xf, xf_v, I_X)
     fetch(neg, neg_buf.at[c, :, pl.ds(0, NEG)], I_NEG)
     fetch(wout, wout_v, I_WOUT)
-    source = p // 2 == s
-
-    @pl.when(source)
-    def _():
-        fetch(w2, w2r_buf.at[p % 2, c], I_W2R)
-
     neg_buf[c, :, NEG:] = jnp.full((1, 128), length, jnp.int32)
     wait(a_buf.at[p, c], here.at[I_W1])
     pl.semaphore_wait(barrier, (G - 1) + (S - 1) + 1)
@@ -254,8 +249,6 @@
         return 0
 
     lax.fori_loop(1, S, at_step, 0)
-    copy(sl2_buf.at[par], sl2_buf.at[par], SL2, pair).start()
-
     wait(b_buf.at[pl.ds(0, C - 1), 0], recv.at[B])
     copy(b_buf.at[:, c], b_buf.at[:, c], BS, sib).start()
 
@@ -269,11 +262,6 @@
     inv[...] = jnp.broadcast_to(item_inverse, inv.shape)
     pe_buf[p] = ui[pl.ds(pl.multiple_of(par * RH, RH), RH)].astype(BF)
     chips(pe_buf.at[p], pe_buf.at[p], PE)
-
-    @pl.when(source)
-    def _():
-        wait(w2r_buf.at[p % 2, c], here.at[I_W2R])
-        chips(w2r_buf.at[p % 2, c], w2r_buf.at[p % 2, c], W2)
 
     wait(wout_v, here.at[I_WOUT])
     wait(at_recv.at[pl.ds(0, S - 1)], recv.at[ATT])
@@ -286,8 +274,7 @@
         [jnp.concatenate(tops, axis=1), jnp.concatenate(bottoms, axis=1)], axis=0).astype(F32)
     branch = (layer_norm(merged) * gate[...].astype(F32)).astype(BF)
     layer_out = (hist_v[...].astype(F32) + dot(branch, wout_v[...])).astype(BF)
-    lo_scr[...] = layer_out
-    pltpu.make_async_copy(lo_scr, lo_ref, here.at[O_LO]).start()
+    lo_ref[...] = layer_out
     outward = layer_out.astype(F32)
     user_inverse = lax.rsqrt(jnp.sum(outward * outward, axis=-1, keepdims=True) + EPS_UNIT)
     unit_user = outward * user_inverse
@@ -305,6 +292,7 @@
     lens = jnp.concatenate([neg_buf[j // 2, :, NEG:] for j in range(4)], axis=1)
     valid = (positions < lens - 1).astype(F32)
 
+    copy(sl2_buf.at[par], sl2_buf.at[par], SL2, pair).start()
     wait(u_buf.at[0], recv.at[UP])
     other = 2 * c + 1 - par
     copy(u_buf.at[other], u_buf.at[other], UT, sib).start()
@@ -340,20 +328,19 @@
     scale = valid / den
 
     for q in range(Q):
-        gq = lax.rem(p // CQ + q, Q)
-        sm = jnp.where(row_id + width * gq == items, slope, scale * em[gq]).astype(BF)
-        st[gq] = sm
-        rs_send[pl.ds(CQ * gq, CQ)] = (TEMP * dot(sm, users)).astype(BF).reshape(CQ, RH, 512)
-
-        def rs_step(i, _):
-            t = CQ * gq + lax.rem(p + i, CQ)
-
-            @pl.when(t != p)
-            def _():
-                copy(rs_send.at[t], rs_recv.at[p], RS, (s, 2 * t + c)).start()
-            return 0
-
-        lax.fori_loop(0, CQ, rs_step, 0)
+        st[q] = jnp.where(row_id + width * q == items, slope, scale * em[q]).astype(BF)
+    half_cols = 256
+
+    def pool_half(e):
+        part = TEMP * dot(st[...].reshape(n_rows, P4), users[:, half_cols * e : half_cols * (e + 1)])
+        rs_send[e] = part.astype(BF).reshape(C, RH, half_cols)
+
+    pool_half(0)
+    chip_scatter(rs_send.at[0], rs_recv.at[0], RS)
+
+    per_block = 128 // (2 * rows)
+    copy(a2_buf.at[pl.ds(per_block * (s + 1 - 2 * par), per_block)], w2r_buf.at[par], W2, pair).start()
+    w2r_buf[par] = a2_buf[pl.ds(per_block * s, per_block)]
 
     mine = quad_pos // tok == me
     loss_sum = jnp.sum(jnp.where(mine, valid * (jnp.log(den) - positive), 0.0))
@@ -367,24 +354,21 @@
     uds_send[...] = ud[1 - c].astype(BF)
     copy(uds_send, uds_recv, UDS, sib).start()
 
-    @pl.when(source)
-    def _():
-        wait(w2r_buf.at[0, 0], recv.at[W2])
-
-    @pl.when(jnp.logical_not(source))
-    def _():
-        wait(w2r_buf.at[:, 0], recv.at[W2])
-
-    copy(w2r_buf.at[:, c], w2r_buf.at[:, c], W2S, sib).start()
+    pool_half(1)
+    wait(rs_recv.at[0, pl.ds(0, C - 1)], send.at[RS])
+    chip_scatter(rs_send.at[1], rs_recv.at[1], RS + 1)
+
+    def plane_sum(e):
+        wait(rs_recv.at[e, pl.ds(0, C - 1)], recv.at[RS + e])
+        za_buf[e, s] = jnp.sum(rs_recv[e].astype(F32), axis=0).astype(BF)
+        z_bcast(za_buf.at[e], ZA + e)
+
+    plane_sum(0)
+    plane_sum(1)
+
     wait(uds_recv, recv.at[UDS])
     udp_send[...] = (ud[c, 1 - par] + uds_recv[1 - par].astype(F32)).astype(BF)
     copy(udp_send, udp_recv, UDP, pair).start()
-
-    wait(rs_recv.at[pl.ds(0, C - 1)], recv.at[RS])
-    rs_recv[p] = rs_send[p]
-    za_buf[s] = jnp.sum(rs_recv[...].astype(F32), axis=0).astype(BF)
-    z_bcast(za_buf, ZA)
-
     wait(zl_buf.at[pl.ds(0, S - 1)], recv.at[ZL])
     lg_buf[g] = jnp.sum(zl_buf[...], axis=0)
 
@@ -393,32 +377,32 @@
         return 0
 
     lax.fori_loop(1, G, lg_step, 0)
-    wait(udp_recv, recv.at[UDP])
-    user_dir = TEMP * (ud[c, par] + uds_recv[par].astype(F32) + udp_recv[...].astype(F32))
-    uun = uu[...]
-    uu[...] = uinv[:, :1] * (user_dir - uun * jnp.sum(uun * user_dir, axis=-1, keepdims=True))
-    pltpu.make_async_copy(uu, ug_ref, here.at[O_UG]).start()
-    wait(w2r_buf.at[:, 0], recv.at[W2S])
+    wait(w2r_buf.at[0], recv.at[W2])
+    w2_rows = jnp.concatenate([w2r_buf[j % 2, :, :, j // 2].reshape(128, 128) for j in range(2 * NB)], axis=1)
     wait(sl2_buf.at[0], recv.at[SL2])
     h1 = jnp.concatenate([h1_buf[j] for j in range(S)], axis=1)
     h2 = whole(h2_buf)
     slope2 = whole(sl2_buf).astype(F32)
     slope1 = silu_slope(pre1[...])
 
-    wait(za_buf.at[pl.ds(0, S - 1)], recv.at[ZA])
-    sums = []
     for e in (0, 1):
-        part = za_buf[e].astype(F32)
-        for t in range(e + 2, S, 2):
-            part = part + za_buf[t].astype(F32)
-        sums.append(part)
-    own_grad = jnp.concatenate(sums, axis=0)
+        wait(za_buf.at[e, pl.ds(0, S - 1)], recv.at[ZA + e])
+    halves = []
+    for e in (0, 1):
+        sums = []
+        for o in (0, 1):
+            part = za_buf[e, o].astype(F32)
+            for t in range(o + 2, S, 2):
+                part = part + za_buf[e, t].astype(F32)
+            sums.append(part)
+        halves.append(jnp.concatenate(sums, axis=0))
+    own_grad = jnp.concatenate(halves, axis=1)
     uin = ui[...]
     raw_grad = (inv[:, :1] * (own_grad - uin * jnp.sum(uin * own_grad, axis=-1, keepdims=True))).astype(BF)
     rg[...] = raw_grad
     sg = (dot_t(raw_grad, b_buf[...].reshape(G * rows, 512)) * slope2).astype(BF)
     sg_scr[...] = sg
-    fg = (dot_t(sg, w2r_buf[...].reshape(4 * rows, 1024)) * slope1).astype(BF)
+    fg = (dot_t(sg, w2_rows) * slope1).astype(BF)
     gp2[...] = t_dot(xf_v[...], fg).astype(BF).reshape(C, 2, rows, 128)
     copy(gp2.at[:, 1 - c], gp2_recv, GP2, sib).start()
     q_cols = pl.ds(pl.multiple_of(lax.rem(s, 4) * 128, 128), 128)
@@ -433,6 +417,10 @@
     g1_send[...] = (gp1[:, c].astype(F32) + gp1_recv[...].astype(F32)).astype(BF)
     chip_scatter(g1_send, g1_recv, G1)
 
+    wait(udp_recv, recv.at[UDP])
+    user_dir = TEMP * (ud[c, par] + uds_recv[par].astype(F32) + udp_recv[...].astype(F32))
+    uun = uu[...]
+    ug_ref[...] = uinv[:, :1] * (user_dir - uun * jnp.sum(uun * user_dir, axis=-1, keepdims=True))
     wait(lg_buf.at[pl.ds(0, G - 1)], recv.at[GL])
     total = jnp.sum(lg_buf[...], axis=0)
     numer = jnp.sum(jnp.where(lane == 0, total, 0.0), axis=1, keepdims=True)
@@ -446,8 +434,6 @@
     f1_buf[s] = jnp.sum(g1_recv[...].astype(F32), axis=0).astype(BF)
     z_bcast(f1_buf, F1)
 
-    pltpu.make_async_copy(lo_scr, lo_ref, here.at[O_LO]).wait()
-    pltpu.make_async_copy(uu, ug_ref, here.at[O_UG]).wait()
     wait(a_buf.at[pl.ds(0, C - 1), 0], send.at[A])
     wait(a2_buf.at[pl.ds(0, C - 1), 0], send.at[A2])
     wait(a2_buf.at[:, 0], send.at[AS2])
@@ -455,8 +441,10 @@
     wait(a_buf.at[:, 0], send.at[AS])
     wait(b_buf.at[:, 0], send.at[BS])
     wait(pe_buf.at[pl.ds(0, C - 1)], send.at[PE])
-    wait(rs_recv.at[pl.ds(0, C - 1)], send.at[RS])
-    for buf, i in ((qr_buf, QKV), (at_recv, ATT), (zl_buf, ZL), (za_buf, ZA)):
+    wait(rs_recv.at[1, pl.ds(0, C - 1)], send.at[RS + 1])
+    for e in (0, 1):
+        wait(za_buf.at[e, pl.ds(0, S - 1)], send.at[ZA + e])
+    for buf, i in ((qr_buf, QKV), (at_recv, ATT), (zl_buf, ZL)):
         wait(buf.at[pl.ds(0, S - 1)], send.at[i])
     wait(h1_buf.at[pl.ds(0, S - 1)], send.at[H1])
     wait(h2_buf.at[0], send.at[H2])
@@ -473,11 +461,7 @@
     wait(lg_buf.at[pl.ds(0, G - 1)], send.at[GL])
     wait(g1_recv.at[pl.ds(0, C - 1)], send.at[G1])
     wait(g2_recv.at[pl.ds(0, C - 1)], send.at[G2])
-    wait(w2r_buf.at[:, 0], send.at[W2S])
-
-    @pl.when(source)
-    def _():
-        wait(b_buf.at[pl.ds(0, C - 1)], send.at[W2])
+    wait(w2r_buf.at[0], send.at[W2])
 
     wait(f2_buf.at[pl.ds(0, S - 1)], recv.at[F2])
     for t in range(S):
@@ -491,18 +475,12 @@
 
 
 def tail(*refs):
-    ins, outs, mids = refs[:6], refs[6:12], refs[12:18]
-    sem = refs[18]
-    for i in range(6):
-        pltpu.make_async_copy(ins[i], mids[i], sem.at[i]).start()
-    for i in range(6):
-        pltpu.make_async_copy(ins[i], mids[i], sem.at[i]).wait()
-        if i == 1:
-            outs[1][0, 0] = jnp.max(mids[1][...])
-        else:
-            pltpu.make_async_copy(mids[i], outs[i], sem.at[6 + i]).start()
+    ins, outs, sem = refs[:6], refs[6:12], refs[12]
     for i in (0, 2, 3, 4, 5):
-        pltpu.make_async_copy(mids[i], outs[i], sem.at[6 + i]).wait()
+        pltpu.make_async_copy(ins[i], outs[i], sem.at[i]).start()
+    outs[1][0, 0] = jnp.max(ins[1][...])
+    for i in (0, 2, 3, 4, 5):
+        pltpu.make_async_copy(ins[i], outs[i], sem.at[i]).wait()
 
 
 def local(history, lengths, next_items, negatives, input_weight, output_weight, pool_features,
@@ -530,7 +508,7 @@
         V((C, 2, rows, 128), BF),
         V((C, 2, 4, rows, 128), BF),
         V((C, 2, rows, 512), BF),
-        V((2, 2, rows, 1024), BF),
+        V((2, 128 // (2 * rows), 2, 4, rows, 128), BF),
         V((S, tok + tok // 2, 128), BF),
         V((S, tok + tok // 2, 128), BF),
         V((tok, 512), BF),
@@ -548,8 +526,8 @@
         V((C, RH, 512), BF),
         V((4, width, 4 * tok), F32),
         V((4, width, 4 * tok), BF),
-        V((C, RH, 512), BF),
-        V((C, RH, 512), BF),
+        V((2, C, RH, 256), BF),
+        V((2, C, RH, 256), BF),
         V((4, tok, 512), BF),
         V((4, 8, 4 * tok), F32),
         V((2, 2, tok, 512), F32),
@@ -557,10 +535,9 @@
         V((2, tok, 512), BF),
         V((tok, 512), BF),
         V((tok, 512), BF),
-        V((tok, 512), BF),
         V((S, 8, 128), F32),
         V((G, 8, 128), F32),
-        V((S, RH, 512), BF),
+        V((2, S, RH, 256), BF),
         V((R, 512), BF),
         V((R, 1024), BF),
         V((C, 2, 2, rows // 2, 128), BF),
@@ -588,9 +565,9 @@
     ]
     results = pl.pallas_call(
         functools.partial(kernel, S, G),
-        out_shape=shapes,
+        out_shape=[pltpu.VMEM(x.shape, x.dtype) for x in shapes],
         in_specs=[pl.BlockSpec(memory_space=pltpu.SMEM)] + [hbm] * 9,
-        out_specs=[hbm, vmem, hbm, vmem, vmem, vmem],
+        out_specs=[vmem] * 6,
         scratch_shapes=scratch,
         compiler_params=pltpu.CompilerParams(
             collective_id=0, has_side_effects=True, vmem_limit_bytes=56 * 1024 * 1024),
@@ -599,10 +576,10 @@
     lo, loss, ug, gf, gm, gl = pl.pallas_call(
         tail,
         out_shape=shapes[:1] + [jax.ShapeDtypeStruct((1, 1), F32)] + shapes[2:],
-        in_specs=[hbm] * 6,
+        in_specs=[vmem] * 6,
         out_specs=[hbm, pl.BlockSpec(memory_space=pltpu.SMEM)] + [hbm] * 4,
-        scratch_shapes=[V(x.shape, x.dtype) for x in shapes] + [pltpu.SemaphoreType.DMA((12,))],
-        compiler_params=pltpu.CompilerParams(vmem_limit_bytes=56 * 1024 * 1024),
+        scratch_shapes=[pltpu.SemaphoreType.DMA((6,))],
+        compiler_params=pltpu.CompilerParams(vmem_limit_bytes=1024 * 1024),
     )(*results)
     return lo[None], loss.reshape(()), ug[None], gf, gm, gl
 

time: 83.5 us -> 77.6 us (0.929)
  Pallas kernels: 82 us -> 76.2 us
    pallas_call x1, Pallas kernels: 79.6 us -> 74.8 us  [local(): pl.pallas_call(functools.partial(kernel, S, G), out_shape=[pltpu.VMEM(x.s...]
    pallas_call x1, Pallas kernels: 2.45 us -> 1.42 us  [local(): pl.pallas_call(tail, out_shape=shapes[:1] + [jax.ShapeDtypeStruct((1, 1),...]
where the time goes in v4:
time: 77.6 us; the launch traced here: 77.5 us
  Pallas kernels  76.2 us (98%)
  between operations  1.29 us (2%)
    pallas_call x1, Pallas kernels, local(): pl.pallas_call(functools.partial(kernel, S, G), out_shape=[pltpu.VMEM(x.s...  74.8 us

profile of v4, /device:TPU:1, one launch (start us, length us, event | category | flops | bytes accessed | tf_op | source)
XLA Modules:
  0.0 77.5 jit_solution(8442854944388236515)
XLA Ops:
  1.3 74.8 %shard_map.145 = (bf16[128,512]{1,0:T(8,128)(2,1)S(1)}, f32[8,128]{1,0:T(8,128)S(1)}, f32[128,512]{1,0:T(8,128)S(1)}, f32[32,1024]{1,0:T(8,128)S(1)}, f32[32,1024]{1,0:T(8,128)S(1)}, /*index=5*/f32[32,512]{1,0:T(8,128)S(1)}) custom-call(s32[1]{0:T(128)S(6)} %copy.16.len_ref, bf16[128,512]{1,0:T(8,128)(2,1)} %bitcast.4, s32[1,128]{1,0:T(1,128)} %nxt.1, ...), custom_call_target="tpu_custom_call" | custom-call | tf_op jit(solution)/shard_map/pallas_call | solution.py:566
  76.0 1.4 %shard_map.146 = (bf16[128,512]{1,0:T(8,128)(2,1)}, f32[1,1]{1,0:T(1,128)}, f32[128,512]{1,0:T(8,128)}, f32[32,1024]{1,0:T(8,128)}, f32[32,1024]{1,0:T(8,128)}, /*index=5*/f32[32,512]{1,0:T(8,128)}) custom-call(bf16[128,512]{1,0:T(8,128)(2,1)S(1)} %get-tuple-element.18.refs_0_, f32[8,128]{1,0:T(8,128)S(1)} %get-tuple-element.19.refs_1_, ...), custom_call_target="tpu_custom_call" | custom-call | tf_op jit(solution)/shard_map/pallas_call | solution.py:576

commit v5 on v4

--- a/solution.py
+++ b/solution.py
@@ -16,10 +16,12 @@
 BF = jnp.bfloat16
 F32 = jnp.float32
 
-(A, A2, B, AS, AS2, BS, QKV, ATT, H1, H2, SL2, NX, NG, UP, US, UT, DN, UDS, UDP, ZL, GL, GP1, GP2, G1, G2, F1, F2,
- W2, PE) = range(29)
-RS, ZA = 29, 31
-N_SEM = 33
+(A, A2, B, AS, AS2, BS, QKV, ATT, H1, H2, SL2, NX, NG, UP, US, UT, DN, UDS, UDP, ZL, GL, GP1, G1, G2, F1, F2,
+ W2, PE) = range(28)
+RS, ZA = 28, 30
+N_SEM = 32
+
+PARTS = ((0, 256), (256, 256))
 
 (I_W3, I_H, I_WIN, I_WOUT, I_X, I_NEG, I_NXT, I_W1) = range(8)
 I_W2 = 8
@@ -65,9 +67,9 @@
     send, recv, here,
     hist_v, nx_buf, neg_buf, win_v, wout_v, xf_v,
     a_buf, a2_buf, b_buf, w2r_buf, qs_buf, qr_buf, gate, k_scr, q_scr, v_scr, at_send, at_recv,
-    h1_buf, h2_buf, sl2_buf, pre1, ui, inv, pe_buf, em, st, rs_send, rs_recv, u_buf,
-    dn_buf, ud, uds_send, uds_recv, udp_send, udp_recv, zl_buf, lg_buf, za_buf, rg, sg_scr,
-    gl_scr, gp1, gp1_recv, gp2, gp2_recv, g1_send, g1_recv, g2_send, g2_recv, f1_buf, f2_buf, cnt, uu, uinv,
+    h1_buf, h2_buf, sl2_buf, pre1, ui, inv, pe_buf, em, st, u_buf,
+    dn_buf, nll, ud, uds_send, uds_recv, udp_send, udp_recv, zl_buf, lg_buf, rg, sg_scr,
+    gl_scr, gp1, gp1_recv, g1_send, g1_recv, g2_send, g2_recv, f1_buf, f2_buf, cnt, uu, uinv, *parts,
 ):
     C = G // 2
     s = lax.axis_index("seq")
@@ -117,6 +119,16 @@
         lax.fori_loop(1, C, step, 0)
         dst[p] = src[p]
 
+    rs_send, rs_recv, za_buf = parts[0:2], parts[2:4], parts[4:6]
+
+    def grp_scatter(src, dst, i):
+        def step(k, _):
+            t = lax.rem(g + k, G)
+            copy(src.at[t], dst.at[g], i, (s, t)).start()
+            return 0
+        lax.fori_loop(1, G, step, 0)
+        dst[g] = src[g]
+
     def quad(buf, i):
         for dev in (sib, pair, diag):
             copy(buf.at[me], buf.at[me], i, dev).start()
@@ -234,6 +246,12 @@
         attend(b)
     at_recv[s] = at_send[s]
 
+    def at_step(k, _):
+        t = lax.rem(s + k, S)
+        copy(at_send.at[t], at_recv.at[s], ATT, (t, g)).start()
+        return 0
+
+    lax.fori_loop(1, S, at_step, 0)
     wait(h1_buf.at[pl.ds(0, S - 1)], recv.at[H1])
     wait(a2_buf.at[:, 0], recv.at[AS2])
     h1 = jnp.concatenate([h1_buf[j] for j in range(S)], axis=1)
@@ -243,12 +261,6 @@
         sl2_buf[par, j] = silu_slope(z2).astype(BF)
     copy(h2_buf.at[par], h2_buf.at[par], H2, pair).start()
 
-    def at_step(k, _):
-        t = lax.rem(s + k, S)
-        copy(at_send.at[t], at_recv.at[s], ATT, (t, g)).start()
-        return 0
-
-    lax.fori_loop(1, S, at_step, 0)
     wait(b_buf.at[pl.ds(0, C - 1), 0], recv.at[B])
     copy(b_buf.at[:, c], b_buf.at[:, c], BS, sib).start()
 
@@ -284,91 +296,104 @@
     uu[...] = unit_user
     uinv[...] = jnp.broadcast_to(user_inverse, (tok, 128))
 
-    P4 = 4 * tok
     wait(nx_buf.at[pl.ds(0, 3)], recv.at[NX])
-    items = local_row(jnp.concatenate([nx_buf[j] for j in range(4)], axis=1))
-    quad_pos = lax.broadcasted_iota(jnp.int32, (1, P4), 1)
-    positions = (s // 2) * W + quad_pos % W
-    lens = jnp.concatenate([neg_buf[j // 2, :, NEG:] for j in range(4)], axis=1)
-    valid = (positions < lens - 1).astype(F32)
+    pair_pos = lax.broadcasted_iota(jnp.int32, (1, W), 1)
+    positions = (s // 2) * W + pair_pos
+
+    def items_of(u):
+        return local_row(jnp.concatenate([nx_buf[2 * u], nx_buf[2 * u + 1]], axis=1))
+
+    def valid_of(u):
+        lens = neg_buf[u, :, NEG:]
+        return (positions < jnp.concatenate([lens, lens], axis=1) - 1).astype(F32)
 
     copy(sl2_buf.at[par], sl2_buf.at[par], SL2, pair).start()
     wait(u_buf.at[0], recv.at[UP])
     other = 2 * c + 1 - par
     copy(u_buf.at[other], u_buf.at[other], UT, sib).start()
     wait(pe_buf.at[pl.ds(0, C - 1)], recv.at[PE])
-    wait(u_buf.at[0], recv.at[US])
-    wait(u_buf.at[0], recv.at[UT])
 
     Q = 4
     CQ = C // Q
     width = n_rows // Q
-    users = u_buf[...].reshape(P4, 512)
-    row_id = lax.broadcasted_iota(jnp.int32, (width, P4), 0)
-    den = jnp.zeros((1, P4), F32)
-    positive = jnp.zeros((1, P4), F32)
-    for q in range(Q):
-        logit = TEMP * dot_t(pe_buf[CQ * q : CQ * (q + 1)].reshape(width, 512), users)
-        own = row_id + width * q == items
-        times = jnp.concatenate([cnt[j // 2, width * q : width * (q + 1)] for j in range(4)], axis=1)
-        e = jnp.where(own, 0.0, jnp.exp(logit) * times)
-        em[q] = e
-        den = den + jnp.sum(e, axis=0, keepdims=True)
-        positive = positive + jnp.sum(jnp.where(own, logit, 0.0), axis=0, keepdims=True)
-    row8 = lax.broadcasted_iota(jnp.int32, (8, P4), 0)
-    dn_buf[me] = jnp.where(row8 == 0, den, positive)
+    row_id = lax.broadcasted_iota(jnp.int32, (width, W), 0)
+
+    def logits_of(u):
+        users = u_buf[pl.ds(2 * u, 2)].reshape(W, 512)
+        items = items_of(u)
+        den = jnp.zeros((1, W), F32)
+        positive = jnp.zeros((1, W), F32)
+        for q in range(Q):
+            logit = TEMP * dot_t(pe_buf[CQ * q : CQ * (q + 1)].reshape(width, 512), users)
+            own = row_id + width * q == items
+            times = cnt[u, width * q : width * (q + 1)]
+            e = jnp.where(own, 0.0, jnp.exp(logit) * jnp.concatenate([times, times], axis=1))
+            em[u, width * q : width * (q + 1)] = e
+            den = den + jnp.sum(e, axis=0, keepdims=True)
+            positive = positive + jnp.sum(jnp.where(own, logit, 0.0), axis=0, keepdims=True)
+        dn_buf[me, u] = jnp.concatenate([den, positive], axis=1)
+
+    logits_of(c)
+    wait(u_buf.at[0], recv.at[US])
+    wait(u_buf.at[0], recv.at[UT])
+    logits_of(1 - c)
     quad(dn_buf, DN)
     wait(dn_buf.at[pl.ds(0, 3)], recv.at[DN])
-    sums = dn_buf[0] + dn_buf[1] + dn_buf[2] + dn_buf[3]
-    den = sums[0:1]
-    positive = sums[1:2]
-    positive_exp = jnp.exp(positive)
-    den = den + positive_exp
-    slope = valid * (positive_exp / den - 1.0)
-    scale = valid / den
-
-    for q in range(Q):
-        st[q] = jnp.where(row_id + width * q == items, slope, scale * em[q]).astype(BF)
-    half_cols = 256
-
-    def pool_half(e):
-        part = TEMP * dot(st[...].reshape(n_rows, P4), users[:, half_cols * e : half_cols * (e + 1)])
-        rs_send[e] = part.astype(BF).reshape(C, RH, half_cols)
-
-    pool_half(0)
-    chip_scatter(rs_send.at[0], rs_recv.at[0], RS)
+    for u in (0, 1):
+        sums = dn_buf[0, u] + dn_buf[1, u] + dn_buf[2, u] + dn_buf[3, u]
+        positive = sums[:, W:]
+        positive_exp = jnp.exp(positive)
+        den = sums[:, :W] + positive_exp
+        valid = valid_of(u)
+        items = items_of(u)
+        slope = valid * (positive_exp / den - 1.0)
+        scale = valid / den
+        for q in range(Q):
+            block = slice(width * q, width * (q + 1))
+            st[u, block] = jnp.where(row_id + width * q == items, slope, scale * em[u, block]).astype(BF)
+        nll[u] = valid * (jnp.log(den) - positive)
+
+    def pool_part(e):
+        lo, n = PARTS[e]
+        part = dot(st[0], u_buf[0:2, :, lo : lo + n].reshape(W, n))
+        part = part + dot(st[1], u_buf[2:4, :, lo : lo + n].reshape(W, n))
+        rs_send[e][...] = (TEMP * part).astype(BF).reshape(C, RH, n)
+
+    pool_part(0)
+    chip_scatter(rs_send[0], rs_recv[0], RS)
 
     per_block = 128 // (2 * rows)
     copy(a2_buf.at[pl.ds(per_block * (s + 1 - 2 * par), per_block)], w2r_buf.at[par], W2, pair).start()
     w2r_buf[par] = a2_buf[pl.ds(per_block * s, per_block)]
 
-    mine = quad_pos // tok == me
-    loss_sum = jnp.sum(jnp.where(mine, valid * (jnp.log(den) - positive), 0.0))
+    mine = pair_pos // tok == par
+    loss_sum = jnp.sum(jnp.where(mine, nll[c], 0.0))
     lane = lax.broadcasted_iota(jnp.int32, (8, 128), 1)
     count = jnp.full((8, 128), length - 1, jnp.int32).astype(F32)
     zl_buf[s] = jnp.where(lane == 0, loss_sum, jnp.where(lane == 1, count, 0.0))
     z_bcast(zl_buf, ZL)
 
-    user_dir = t_dot(st[...].reshape(n_rows, P4), pe_buf[...].reshape(n_rows, 512))
-    ud[...] = user_dir.reshape(2, 2, tok, 512)
+    rows_here = pe_buf[...].reshape(n_rows, 512)
+    for u in (0, 1):
+        ud[u] = t_dot(st[u], rows_here).reshape(2, tok, 512)
     uds_send[...] = ud[1 - c].astype(BF)
     copy(uds_send, uds_recv, UDS, sib).start()
 
-    pool_half(1)
-    wait(rs_recv.at[0, pl.ds(0, C - 1)], send.at[RS])
-    chip_scatter(rs_send.at[1], rs_recv.at[1], RS + 1)
+    pool_part(1)
+    wait(rs_recv[0].at[pl.ds(0, C - 1)], send.at[RS])
+    chip_scatter(rs_send[1], rs_recv[1], RS + 1)
 
     def plane_sum(e):
-        wait(rs_recv.at[e, pl.ds(0, C - 1)], recv.at[RS + e])
-        za_buf[e, s] = jnp.sum(rs_recv[e].astype(F32), axis=0).astype(BF)
-        z_bcast(za_buf.at[e], ZA + e)
+        wait(rs_recv[e].at[pl.ds(0, C - 1)], recv.at[RS + e])
+        za_buf[e][s] = jnp.sum(rs_recv[e][...].astype(F32), axis=0).astype(BF)
+        z_bcast(za_buf[e], ZA + e)
 
     plane_sum(0)
     plane_sum(1)
-
     wait(uds_recv, recv.at[UDS])
     udp_send[...] = (ud[c, 1 - par] + uds_recv[1 - par].astype(F32)).astype(BF)
     copy(udp_send, udp_recv, UDP, pair).start()
+
     wait(zl_buf.at[pl.ds(0, S - 1)], recv.at[ZL])
     lg_buf[g] = jnp.sum(zl_buf[...], axis=0)
 
@@ -385,34 +410,31 @@
     slope2 = whole(sl2_buf).astype(F32)
     slope1 = silu_slope(pre1[...])
 
-    for e in (0, 1):
-        wait(za_buf.at[e, pl.ds(0, S - 1)], recv.at[ZA + e])
-    halves = []
-    for e in (0, 1):
+    for e in range(2):
+        wait(za_buf[e].at[pl.ds(0, S - 1)], recv.at[ZA + e])
+    chunks = []
+    for e in range(2):
         sums = []
         for o in (0, 1):
-            part = za_buf[e, o].astype(F32)
+            part = za_buf[e][o].astype(F32)
             for t in range(o + 2, S, 2):
-                part = part + za_buf[e, t].astype(F32)
+                part = part + za_buf[e][t].astype(F32)
             sums.append(part)
-        halves.append(jnp.concatenate(sums, axis=0))
-    own_grad = jnp.concatenate(halves, axis=1)
+        chunks.append(jnp.concatenate(sums, axis=0))
+    own_grad = jnp.concatenate(chunks, axis=1)
     uin = ui[...]
     raw_grad = (inv[:, :1] * (own_grad - uin * jnp.sum(uin * own_grad, axis=-1, keepdims=True))).astype(BF)
     rg[...] = raw_grad
     sg = (dot_t(raw_grad, b_buf[...].reshape(G * rows, 512)) * slope2).astype(BF)
     sg_scr[...] = sg
     fg = (dot_t(sg, w2_rows) * slope1).astype(BF)
-    gp2[...] = t_dot(xf_v[...], fg).astype(BF).reshape(C, 2, rows, 128)
-    copy(gp2.at[:, 1 - c], gp2_recv, GP2, sib).start()
+    g2_send[...] = t_dot(xf_v[...], fg).astype(BF).reshape(G, rows, 128)
+    grp_scatter(g2_send, g2_recv, G2)
     q_cols = pl.ds(pl.multiple_of(lax.rem(s, 4) * 128, 128), 128)
     gl_scr[...] = t_dot(h2, rg[:, q_cols]).astype(BF).reshape(C, 2, 2, half, 128)
     gp1[:, :, :rows] = t_dot(h1, sg_scr[:, cols]).astype(BF).reshape(C, 2, rows, 128)
     gp1[:, :, rows:] = gl_scr[:, :, s // 4]
     copy(gp1.at[:, 1 - c], gp1_recv, GP1, sib).start()
-    wait(gp2_recv, recv.at[GP2])
-    g2_send[...] = (gp2[:, c].astype(F32) + gp2_recv[...].astype(F32)).astype(BF)
-    chip_scatter(g2_send, g2_recv, G2)
     wait(gp1_recv, recv.at[GP1])
     g1_send[...] = (gp1[:, c].astype(F32) + gp1_recv[...].astype(F32)).astype(BF)
     chip_scatter(g1_send, g1_recv, G1)
@@ -427,7 +449,7 @@
     denom = jnp.sum(jnp.where(lane == 1, total, 0.0), axis=1, keepdims=True)
     loss_ref[...] = jnp.broadcast_to(numer * S / denom, loss_ref.shape)
 
-    wait(g2_recv.at[pl.ds(0, C - 1)], recv.at[G2])
+    wait(g2_recv.at[pl.ds(0, G - 1)], recv.at[G2])
     f2_buf[s] = jnp.sum(g2_recv[...].astype(F32), axis=0).astype(BF)
     z_bcast(f2_buf, F2)
     wait(g1_recv.at[pl.ds(0, C - 1)], recv.at[G1])
@@ -441,9 +463,9 @@
     wait(a_buf.at[:, 0], send.at[AS])
     wait(b_buf.at[:, 0], send.at[BS])
     wait(pe_buf.at[pl.ds(0, C - 1)], send.at[PE])
-    wait(rs_recv.at[1, pl.ds(0, C - 1)], send.at[RS + 1])
-    for e in (0, 1):
-        wait(za_buf.at[e, pl.ds(0, S - 1)], send.at[ZA + e])
+    wait(rs_recv[1].at[pl.ds(0, C - 1)], send.at[RS + 1])
+    for e in range(2):
+        wait(za_buf[e].at[pl.ds(0, S - 1)], send.at[ZA + e])
     for buf, i in ((qr_buf, QKV), (at_recv, ATT), (zl_buf, ZL)):
         wait(buf.at[pl.ds(0, S - 1)], send.at[i])
     wait(h1_buf.at[pl.ds(0, S - 1)], send.at[H1])
@@ -457,10 +479,9 @@
     wait(uds_recv, send.at[UDS])
     wait(udp_recv, send.at[UDP])
     wait(gp1_recv, send.at[GP1])
-    wait(gp2_recv, send.at[GP2])
     wait(lg_buf.at[pl.ds(0, G - 1)], send.at[GL])
     wait(g1_recv.at[pl.ds(0, C - 1)], send.at[G1])
-    wait(g2_recv.at[pl.ds(0, C - 1)], send.at[G2])
+    wait(g2_recv.at[pl.ds(0, G - 1)], send.at[G2])
     wait(w2r_buf.at[0], send.at[W2])
 
     wait(f2_buf.at[pl.ds(0, S - 1)], recv.at[F2])
@@ -494,7 +515,6 @@
     V = pltpu.VMEM
     vmem = pl.BlockSpec(memory_space=pltpu.VMEM)
     hbm = pl.BlockSpec(memory_space=pltpu.HBM)
-    width = C * RH // 4
     scratch = [
         pltpu.SemaphoreType.DMA((N_SEM,)),
         pltpu.SemaphoreType.DMA((N_SEM,)),
@@ -524,12 +544,11 @@
         V((R, 512), F32),
         V((R, 128), F32),
         V((C, RH, 512), BF),
-        V((4, width, 4 * tok), F32),
-        V((4, width, 4 * tok), BF),
-        V((2, C, RH, 256), BF),
-        V((2, C, RH, 256), BF),
+        V((2, C * RH, 2 * tok), F32),
+        V((2, C * RH, 2 * tok), BF),
         V((4, tok, 512), BF),
-        V((4, 8, 4 * tok), F32),
+        V((4, 2, 1, 4 * tok), F32),
+        V((2, 1, 2 * tok), F32),
         V((2, 2, tok, 512), F32),
         V((2, tok, 512), BF),
         V((2, tok, 512), BF),
@@ -537,24 +556,23 @@
         V((tok, 512), BF),
         V((S, 8, 128), F32),
         V((G, 8, 128), F32),
-        V((2, S, RH, 256), BF),
         V((R, 512), BF),
         V((R, 1024), BF),
         V((C, 2, 2, rows // 2, 128), BF),
         V((C, 2, rows + rows // 2, 128), BF),
         V((C, rows + rows // 2, 128), BF),
-        V((C, 2, rows, 128), BF),
-        V((C, rows, 128), BF),
         V((C, rows + rows // 2, 128), BF),
         V((C, rows + rows // 2, 128), BF),
-        V((C, rows, 128), BF),
-        V((C, rows, 128), BF),
+        V((G, rows, 128), BF),
+        V((G, rows, 128), BF),
         V((S, rows + rows // 2, 128), BF),
         V((S, rows, 128), BF),
         V((2, C * RH, 128), F32),
         V((tok, 512), F32),
         V((tok, 128), F32),
     ]
+    for lead in (C, C, S):
+        scratch += [V((lead, RH, n), BF) for _, n in PARTS]
     shapes = [
         jax.ShapeDtypeStruct((tok, 512), BF),
         jax.ShapeDtypeStruct((8, 128), F32),

time: 77.6 us -> 76.4 us (0.985)
  Pallas kernels: 76.2 us -> 74.9 us
    pallas_call x1, Pallas kernels: 74.8 us -> 73.5 us  [local(): pl.pallas_call(functools.partial(kernel, S, G), out_shape=[pltpu.VMEM(x.s...]
where the time goes in v5:
time: 76.4 us; the launch traced here: 76.2 us
  Pallas kernels  74.9 us (98%)
  between operations  1.29 us (2%)
    pallas_call x1, Pallas kernels, local(): pl.pallas_call(functools.partial(kernel, S, G), out_shape=[pltpu.VMEM(x.s...  73.5 us

profile of v5, /device:TPU:1, one launch (start us, length us, event | category | flops | bytes accessed | tf_op | source)
XLA Modules:
  0.0 76.2 jit_solution(350421947815061175)
XLA Ops:
  1.3 73.5 %shard_map.145 = (bf16[128,512]{1,0:T(8,128)(2,1)S(1)}, f32[8,128]{1,0:T(8,128)S(1)}, f32[128,512]{1,0:T(8,128)S(1)}, f32[32,1024]{1,0:T(8,128)S(1)}, f32[32,1024]{1,0:T(8,128)S(1)}, /*index=5*/f32[32,512]{1,0:T(8,128)S(1)}) custom-call(s32[1]{0:T(128)S(6)} %copy.16.len_ref, bf16[128,512]{1,0:T(8,128)(2,1)} %bitcast.4, s32[1,128]{1,0:T(1,128)} %nxt.1, ...), custom_call_target="tpu_custom_call" | custom-call | tf_op jit(solution)/shard_map/pallas_call | solution.py:584
  74.8 1.4 %shard_map.146 = (bf16[128,512]{1,0:T(8,128)(2,1)}, f32[1,1]{1,0:T(1,128)}, f32[128,512]{1,0:T(8,128)}, f32[32,1024]{1,0:T(8,128)}, f32[32,1024]{1,0:T(8,128)}, /*index=5*/f32[32,512]{1,0:T(8,128)}) custom-call(bf16[128,512]{1,0:T(8,128)(2,1)S(1)} %get-tuple-element.18.refs_0_, f32[8,128]{1,0:T(8,128)S(1)} %get-tuple-element.19.refs_1_, ...), custom_call_target="tpu_custom_call" | custom-call | tf_op jit(solution)/shard_map/pallas_call | solution.py:594

commit v6 on v5

--- a/solution.py
+++ b/solution.py
@@ -307,7 +307,6 @@
         lens = neg_buf[u, :, NEG:]
         return (positions < jnp.concatenate([lens, lens], axis=1) - 1).astype(F32)
 
-    copy(sl2_buf.at[par], sl2_buf.at[par], SL2, pair).start()
     wait(u_buf.at[0], recv.at[UP])
     other = 2 * c + 1 - par
     copy(u_buf.at[other], u_buf.at[other], UT, sib).start()
@@ -365,6 +364,7 @@
     per_block = 128 // (2 * rows)
     copy(a2_buf.at[pl.ds(per_block * (s + 1 - 2 * par), per_block)], w2r_buf.at[par], W2, pair).start()
     w2r_buf[par] = a2_buf[pl.ds(per_block * s, per_block)]
+    copy(sl2_buf.at[par], sl2_buf.at[par], SL2, pair).start()
 
     mine = pair_pos // tok == par
     loss_sum = jnp.sum(jnp.where(mine, nll[c], 0.0))
@@ -390,10 +390,6 @@
 
     plane_sum(0)
     plane_sum(1)
-    wait(uds_recv, recv.at[UDS])
-    udp_send[...] = (ud[c, 1 - par] + uds_recv[1 - par].astype(F32)).astype(BF)
-    copy(udp_send, udp_recv, UDP, pair).start()
-
     wait(zl_buf.at[pl.ds(0, S - 1)], recv.at[ZL])
     lg_buf[g] = jnp.sum(zl_buf[...], axis=0)
 
@@ -435,14 +431,13 @@
     gp1[:, :, :rows] = t_dot(h1, sg_scr[:, cols]).astype(BF).reshape(C, 2, rows, 128)
     gp1[:, :, rows:] = gl_scr[:, :, s // 4]
     copy(gp1.at[:, 1 - c], gp1_recv, GP1, sib).start()
+    wait(uds_recv, recv.at[UDS])
+    udp_send[...] = (ud[c, 1 - par] + uds_recv[1 - par].astype(F32)).astype(BF)
+    copy(udp_send, udp_recv, UDP, pair).start()
     wait(gp1_recv, recv.at[GP1])
     g1_send[...] = (gp1[:, c].astype(F32) + gp1_recv[...].astype(F32)).astype(BF)
     chip_scatter(g1_send, g1_recv, G1)
 
-    wait(udp_recv, recv.at[UDP])
-    user_dir = TEMP * (ud[c, par] + uds_recv[par].astype(F32) + udp_recv[...].astype(F32))
-    uun = uu[...]
-    ug_ref[...] = uinv[:, :1] * (user_dir - uun * jnp.sum(uun * user_dir, axis=-1, keepdims=True))
     wait(lg_buf.at[pl.ds(0, G - 1)], recv.at[GL])
     total = jnp.sum(lg_buf[...], axis=0)
     numer = jnp.sum(jnp.where(lane == 0, total, 0.0), axis=1, keepdims=True)
@@ -456,6 +451,10 @@
     f1_buf[s] = jnp.sum(g1_recv[...].astype(F32), axis=0).astype(BF)
     z_bcast(f1_buf, F1)
 
+    wait(udp_recv, recv.at[UDP])
+    user_dir = TEMP * (ud[c, par] + uds_recv[par].astype(F32) + udp_recv[...].astype(F32))
+    uun = uu[...]
+    ug_ref[...] = uinv[:, :1] * (user_dir - uun * jnp.sum(uun * user_dir, axis=-1, keepdims=True))
     wait(a_buf.at[pl.ds(0, C - 1), 0], send.at[A])
     wait(a2_buf.at[pl.ds(0, C - 1), 0], send.at[A2])
     wait(a2_buf.at[:, 0], send.at[AS2])

time: 76.4 us -> 75.7 us (level)
  no operation moved by 1% of the time
where the time goes in v6:
time: 75.7 us; the launch traced here: 75.6 us
  Pallas kernels  74.3 us (98%)
  between operations  1.29 us (2%)
    pallas_call x1, Pallas kernels, local(): pl.pallas_call(functools.partial(kernel, S, G), out_shape=[pltpu.VMEM(x.s...  72.9 us

profile of v6, /device:TPU:1, one launch (start us, length us, event | category | flops | bytes accessed | tf_op | source)
XLA Modules:
  0.0 75.6 jit_solution(4330973458418467017)
XLA Ops:
  1.3 72.9 %shard_map.145 = (bf16[128,512]{1,0:T(8,128)(2,1)S(1)}, f32[8,128]{1,0:T(8,128)S(1)}, f32[128,512]{1,0:T(8,128)S(1)}, f32[32,1024]{1,0:T(8,128)S(1)}, f32[32,1024]{1,0:T(8,128)S(1)}, /*index=5*/f32[32,512]{1,0:T(8,128)S(1)}) custom-call(s32[1]{0:T(128)S(6)} %copy.16.len_ref, bf16[128,512]{1,0:T(8,128)(2,1)} %bitcast.4, s32[1,128]{1,0:T(1,128)} %nxt.1, ...), custom_call_target="tpu_custom_call" | custom-call | tf_op jit(solution)/shard_map/pallas_call | solution.py:583
  74.2 1.4 %shard_map.146 = (bf16[128,512]{1,0:T(8,128)(2,1)}, f32[1,1]{1,0:T(1,128)}, f32[128,512]{1,0:T(8,128)}, f32[32,1024]{1,0:T(8,128)}, f32[32,1024]{1,0:T(8,128)}, /*index=5*/f32[32,512]{1,0:T(8,128)}) custom-call(bf16[128,512]{1,0:T(8,128)(2,1)S(1)} %get-tuple-element.18.refs_0_, f32[8,128]{1,0:T(8,128)S(1)} %get-tuple-element.19.refs_1_, ...), custom_call_target="tpu_custom_call" | custom-call | tf_op jit(solution)/shard_map/pallas_call | solution.py:593

commit v7 on v6

--- a/solution.py
+++ b/solution.py
@@ -99,11 +99,14 @@
     def fetch(src, dst, i):
         pltpu.make_async_copy(src, dst, here.at[i]).start()
 
+    def z_away(i):
+        return lax.rem(s + S // 2 + (1 - 2 * (i % 2)) * ((i + 1) // 2), S)
+
     def z_bcast(buf, i):
         def step(k, _):
-            copy(buf.at[s], buf.at[s], i, (lax.rem(s + k, S), g)).start()
+            copy(buf.at[s], buf.at[s], i, (z_away(k), g)).start()
             return 0
-        lax.fori_loop(1, S, step, 0)
+        lax.fori_loop(0, S - 1, step, 0)
 
     def chips(src, dst, i):
         def step(k, _):
@@ -175,11 +178,11 @@
             qs_buf[2 * j + e, tok:] = jnp.concatenate([v[: tok // 2], v[tok // 2 :]], axis=1)
 
     def qkv_step(k, _):
-        t = lax.rem(s + k, S)
+        t = z_away(k)
         copy(qs_buf.at[t], qr_buf.at[s], QKV, (t, g)).start()
         return 0
 
-    lax.fori_loop(1, S, qkv_step, 0)
+    lax.fori_loop(0, S - 1, qkv_step, 0)
     qr_buf[s] = qs_buf[s]
     for j in range(NB):
         wait(a2_buf.at[p, c, j], here.at[I_W2 + j])
@@ -247,11 +250,11 @@
     at_recv[s] = at_send[s]
 
     def at_step(k, _):
-        t = lax.rem(s + k, S)
+        t = z_away(k)
         copy(at_send.at[t], at_recv.at[s], ATT, (t, g)).start()
         return 0
 
-    lax.fori_loop(1, S, at_step, 0)
+    lax.fori_loop(0, S - 1, at_step, 0)
     wait(h1_buf.at[pl.ds(0, S - 1)], recv.at[H1])
     wait(a2_buf.at[:, 0], recv.at[AS2])
     h1 = jnp.concatenate([h1_buf[j] for j in range(S)], axis=1)

time: 75.7 us -> 73.6 us (0.972)
  Pallas kernels: 74.3 us -> 72.2 us
    pallas_call x1, Pallas kernels: 72.9 us -> 70.7 us  [local(): pl.pallas_call(functools.partial(kernel, S, G), out_shape=[pltpu.VMEM(x.s...]
where the time goes in v7:
time: 73.6 us; the launch traced here: 73.4 us
  Pallas kernels  72.2 us (98%)
  between operations  1.29 us (2%)
    pallas_call x1, Pallas kernels, local(): pl.pallas_call(functools.partial(kernel, S, G), out_shape=[pltpu.VMEM(x.s...  70.7 us

profile of v7, /device:TPU:1, one launch (start us, length us, event | category | flops | bytes accessed | tf_op | source)
XLA Modules:
  0.0 73.4 jit_solution(410063640892345274)
XLA Ops:
  1.3 70.7 %shard_map.145 = (bf16[128,512]{1,0:T(8,128)(2,1)S(1)}, f32[8,128]{1,0:T(8,128)S(1)}, f32[128,512]{1,0:T(8,128)S(1)}, f32[32,1024]{1,0:T(8,128)S(1)}, f32[32,1024]{1,0:T(8,128)S(1)}, /*index=5*/f32[32,512]{1,0:T(8,128)S(1)}) custom-call(s32[1]{0:T(128)S(6)} %copy.16.len_ref, bf16[128,512]{1,0:T(8,128)(2,1)} %bitcast.4, s32[1,128]{1,0:T(1,128)} %nxt.1, ...), custom_call_target="tpu_custom_call" | custom-call | tf_op jit(solution)/shard_map/pallas_call | solution.py:586
  72.0 1.4 %shard_map.146 = (bf16[128,512]{1,0:T(8,128)(2,1)}, f32[1,1]{1,0:T(1,128)}, f32[128,512]{1,0:T(8,128)}, f32[32,1024]{1,0:T(8,128)}, f32[32,1024]{1,0:T(8,128)}, /*index=5*/f32[32,512]{1,0:T(8,128)}) custom-call(bf16[128,512]{1,0:T(8,128)(2,1)S(1)} %get-tuple-element.18.refs_0_, f32[8,128]{1,0:T(8,128)S(1)} %get-tuple-element.19.refs_1_, ...), custom_call_target="tpu_custom_call" | custom-call | tf_op jit(solution)/shard_map/pallas_call | solution.py:596

commit v8 on v7

--- a/solution.py
+++ b/solution.py
@@ -144,11 +144,12 @@
         return 0
 
     def greet_seq(k, _):
-        pl.semaphore_signal(barrier, inc=1, device_id=(lax.rem(s + k, S), g), device_id_type=MESH)
+        pl.semaphore_signal(barrier, inc=1, device_id=(z_away(k), g), device_id_type=MESH)
         return 0
 
-    lax.fori_loop(1, G, greet_grp, 0)
-    lax.fori_loop(1, S, greet_seq, 0)
+    lax.fori_loop(0, S - 1, greet_seq, 0)
+    lax.fori_loop(G // 2, G, greet_grp, 0)
+    lax.fori_loop(1, G // 2, greet_grp, 0)
     pl.semaphore_signal(barrier, inc=1, device_id=diag, device_id_type=MESH)
 
     for j in range(NB):

time: 73.6 us -> 74.1 us (level)
  no operation moved by 1% of the time
where the time goes in v8:
time: 74.1 us; the launch traced here: 74 us
  Pallas kernels  72.7 us (98%)
  between operations  1.29 us (2%)
    pallas_call x1, Pallas kernels, local(): pl.pallas_call(functools.partial(kernel, S, G), out_shape=[pltpu.VMEM(x.s...  71.2 us

profile of v8, /device:TPU:1, one launch (start us, length us, event | category | flops | bytes accessed | tf_op | source)
XLA Modules:
  0.0 74.0 jit_solution(16820004759049106054)
XLA Ops:
  1.3 71.2 %shard_map.145 = (bf16[128,512]{1,0:T(8,128)(2,1)S(1)}, f32[8,128]{1,0:T(8,128)S(1)}, f32[128,512]{1,0:T(8,128)S(1)}, f32[32,1024]{1,0:T(8,128)S(1)}, f32[32,1024]{1,0:T(8,128)S(1)}, /*index=5*/f32[32,512]{1,0:T(8,128)S(1)}) custom-call(s32[1]{0:T(128)S(6)} %copy.16.len_ref, bf16[128,512]{1,0:T(8,128)(2,1)} %bitcast.4, s32[1,128]{1,0:T(1,128)} %nxt.1, ...), custom_call_target="tpu_custom_call" | custom-call | tf_op jit(solution)/shard_map/pallas_call | solution.py:587
  72.5 1.4 %shard_map.146 = (bf16[128,512]{1,0:T(8,128)(2,1)}, f32[1,1]{1,0:T(1,128)}, f32[128,512]{1,0:T(8,128)}, f32[32,1024]{1,0:T(8,128)}, f32[32,1024]{1,0:T(8,128)}, /*index=5*/f32[32,512]{1,0:T(8,128)}) custom-call(bf16[128,512]{1,0:T(8,128)(2,1)S(1)} %get-tuple-element.18.refs_0_, f32[8,128]{1,0:T(8,128)S(1)} %get-tuple-element.19.refs_1_, ...), custom_call_target="tpu_custom_call" | custom-call | tf_op jit(solution)/shard_map/pallas_call | solution.py:597

commit v9 on v7

--- a/solution.py
+++ b/solution.py
@@ -108,18 +108,25 @@
             return 0
         lax.fori_loop(0, S - 1, step, 0)
 
+    def chip_away(k):
+        return (p // 4 + 2 + k // 4) % 4 * 4 + (p + 2 + k) % 4
+
+    def each_chip(step):
+        lax.fori_loop(0, 10, step, 0)
+        lax.fori_loop(11, 16, step, 0)
+
     def chips(src, dst, i):
         def step(k, _):
-            copy(src, dst, i, (s, 2 * lax.rem(p + k, C) + c)).start()
+            copy(src, dst, i, (s, 2 * chip_away(k) + c)).start()
             return 0
-        lax.fori_loop(1, C, step, 0)
+        each_chip(step)
 
     def chip_scatter(src, dst, i):
         def step(k, _):
-            t = lax.rem(p + k, C)
+            t = chip_away(k)
             copy(src.at[t], dst.at[p], i, (s, 2 * t + c)).start()
             return 0
-        lax.fori_loop(1, C, step, 0)
+        each_chip(step)
         dst[p] = src[p]
 
     rs_send, rs_recv, za_buf = parts[0:2], parts[2:4], parts[4:6]

time: 73.6 us -> 74.7 us (1.015)
  Pallas kernels: 72.2 us -> 73.4 us
    pallas_call x1, Pallas kernels: 70.7 us -> 72 us  [local(): pl.pallas_call(functools.partial(kernel, S, G), out_shape=[pltpu.VMEM(x.s...]
where the time goes in v9:
time: 74.7 us
  Pallas kernels  73.4 us (98%)
  between operations  1.29 us (2%)
    pallas_call x1, Pallas kernels, local(): pl.pallas_call(functools.partial(kernel, S, G), out_shape=[pltpu.VMEM(x.s...  72 us

profile of v9, /device:TPU:1, one launch (start us, length us, event | category | flops | bytes accessed | tf_op | source)
XLA Modules:
  0.0 74.7 jit_solution(10126854290707624323)
XLA Ops:
  1.3 72.0 %shard_map.145 = (bf16[128,512]{1,0:T(8,128)(2,1)S(1)}, f32[8,128]{1,0:T(8,128)S(1)}, f32[128,512]{1,0:T(8,128)S(1)}, f32[32,1024]{1,0:T(8,128)S(1)}, f32[32,1024]{1,0:T(8,128)S(1)}, /*index=5*/f32[32,512]{1,0:T(8,128)S(1)}) custom-call(s32[1]{0:T(128)S(6)} %copy.16.len_ref, bf16[128,512]{1,0:T(8,128)(2,1)} %bitcast.4, s32[1,128]{1,0:T(1,128)} %nxt.1, ...), custom_call_target="tpu_custom_call" | custom-call | tf_op jit(solution)/shard_map/pallas_call | solution.py:593
  73.3 1.4 %shard_map.146 = (bf16[128,512]{1,0:T(8,128)(2,1)}, f32[1,1]{1,0:T(1,128)}, f32[128,512]{1,0:T(8,128)}, f32[32,1024]{1,0:T(8,128)}, f32[32,1024]{1,0:T(8,128)}, /*index=5*/f32[32,512]{1,0:T(8,128)}) custom-call(bf16[128,512]{1,0:T(8,128)(2,1)S(1)} %get-tuple-element.18.refs_0_, f32[8,128]{1,0:T(8,128)S(1)} %get-tuple-element.19.refs_1_, ...), custom_call_target="tpu_custom_call" | custom-call | tf_op jit(solution)/shard_map/pallas_call | solution.py:603
